TPU v7x, 32 devices: a whole 2x2x4 slice. The times are simulated.
32 devices in a mesh: leaf: 4 (over x, core), blk: 8 (over z, y).
Axes of the slice: x: 2, y: 2, z: 4, core: 2. Of those that a mesh axis runs over, the one named last changes fastest.
Arguments:
- interior_factor: float32 [32, 256, 256], P(('leaf', 'blk')), may hold values from -0.375 to 0.375
- coupling: float32 [32, 64, 256], P(('leaf', 'blk')), may hold values from -2 to 2
- iface_rows: int32 [32, 64], P(('leaf', 'blk')), may hold values from 0 to 1535, as said below
- counts: int32 [32], P(('leaf', 'blk')), may hold values from 16 to 64, as said below
- resid_interior: float32 [32, 256], P(('leaf', 'blk')), may hold values from -6 to 6
- resid_iface: float32 [1536], replicated, may hold values from -6 to 6
- iface_operator: float32 [1536, 1536], replicated, as said below
Outputs:
- interior_solution: float32 [32, 256], P(('leaf', 'blk'))
- iface_solution: float32 [1536], P('blk')
Inputs may be any that keep to these rules, and one draw needn't show every extreme that they name: `iface_rows`: the 64 rows of one block's list are distinct. `counts`: some block uses 64 rows and some block uses 64 // 4. `iface_operator`: symmetric positive definite.
All inputs are finite; a program needn't handle non-finite values.
Results may differ from a plain program's by a relative error of at most 0.0002.
Values sent between devices are 32-bit elements; how exact they have to be, the bound alone decides.
No kernel may reach another device: no remote copies, remote signals or barrier semaphores. Data moves between devices by JAX's collectives and lax.ppermute only.
A program may use at most 128 MiB of HBM per device.

v0:
```python
import jax
import jax.numpy as jnp
from jax import lax
from jax.sharding import PartitionSpec as P


def joined(part, axis, combine):
    gathered = jax.tree.map(lambda a: lax.all_gather(a, axis), part)

    def take(source):
        return jax.tree.map(lambda a: lax.dynamic_index_in_dim(a, source, 0, False), gathered)

    return lax.fori_loop(
        1, lax.axis_size(axis), lambda source, state: combine(state, take(source)), take(0)
    )


def add_pair(first, second):
    return (first[0] + second[0], first[1] + second[1])


def shards(
    interior_factor, coupling, iface_rows, counts, resid_interior, resid_iface, iface_operator
):
    highest = lax.Precision.HIGHEST
    factor = interior_factor[0]
    couple = coupling[0]
    row_list = iface_rows[0]
    row_count = counts[0]
    capacity = couple.shape[0]
    active = (jnp.arange(capacity, dtype=jnp.int32) < row_count).astype(jnp.float32)
    coupled = couple * active[:, None]
    reduced = jnp.dot(coupled, factor.T, precision=highest)
    local_rhs = jnp.dot(factor, resid_interior[0], precision=highest)
    piece = jnp.dot(reduced, reduced.T, precision=highest)
    piece_rhs = jnp.dot(reduced, local_rhs, precision=highest)
    order = iface_operator.shape[0]
    dense_term = (
        jnp.zeros((order, order), jnp.float32).at[row_list[:, None], row_list[None, :]].add(piece)
    )
    dense_rhs = jnp.zeros((order,), jnp.float32).at[row_list].add(piece_rhs)
    share_rows, share_rhs = (
        lax.psum_scatter(dense_term, "blk", scatter_dimension=0, tiled=True),
        lax.psum_scatter(dense_rhs, "blk", scatter_dimension=0, tiled=True),
    )
    share_rows, share_rhs = joined((share_rows, share_rhs), "leaf", add_pair)
    whole_sum, whole_rhs = (
        lax.all_gather(share_rows, "blk", axis=0, tiled=True),
        lax.all_gather(share_rhs, "blk", axis=0, tiled=True),
    )
    schur_matrix = iface_operator + whole_sum
    iface_rhs = resid_iface + whole_rhs
    lower_factor = jnp.linalg.cholesky(schur_matrix)
    solution = jax.scipy.linalg.cho_solve((lower_factor, True), iface_rhs)
    picked = solution[row_list]
    corrected = resid_interior[0] - jnp.dot(picked, coupled, precision=highest)
    inner_values = jnp.dot(factor, corrected, precision=highest)
    interior = jnp.dot(inner_values, factor, precision=highest)
    own_rows = order // lax.axis_size("blk")
    own_part = lax.dynamic_slice_in_dim(solution, lax.axis_index("blk") * own_rows, own_rows, 0)
    return (interior[None], own_part)


def solution(mesh):
    return jax.shard_map(
        shards,
        mesh=mesh,
        in_specs=(
            P(("leaf", "blk"), None, None),
            P(("leaf", "blk"), None, None),
            P(("leaf", "blk"), None),
            P(("leaf", "blk")),
            P(("leaf", "blk"), None),
            P(),
            P(),
        ),
        out_specs=(P(("leaf", "blk"), None), P("blk")),
        check_vma=False,
    )
```

profile of v0, /device:TPU:0, one launch (start us, length us, event | category | flops | bytes accessed | tf_op | source)
XLA Modules:
  0.0 979.0 jit_solution(9766382895016507416)
XLA Ops:
  11.7 26.5 %scatter_custom_fusion.1 = f32[2359296]{0:T(1024)} fusion(s32[4096]{0:T(1024)S(1)} %reshape.467, f32[4096]{0:T(1024)S(1)} %reshape.469, f32[]{:T(128)} %constant.466.clone.1), kind=kCustom, calls=%fused_computation.11 | custom fusion | flops 4096 | bytes 9437188
  38.2 11.0 %reshape.427 = f32[1536,1536]{1,0:T(8,128)} reshape(f32[2359296]{0:T(1024)} %scatter_custom_fusion.1) | data formatting | bytes 18874368 | tf_op jit(solution)/shard_map/scatter-add | solution.py:39
  49.3 166.0 %reduce-scatter.2.cloned.1.call-done = f32[192,1536]{1,0:T(8,128)} async-done(((f32[1536,1536]{1,0:T(8,128)}), f32[192,1536]{1,0:T(8,128)}) %reduce-scatter.2.cloned.1.call-update) | async-done | bytes 1179664 | tf_op jit(solution)/shard_map/reduce_scatter | solution.py:43
  219.4 19.7 %all-reduce.3 = f32[1536]{0:T(1024)S(1)} all-reduce(f32[1536]{0:T(1024)S(1)} %scatter_custom_fusion), channel_id=5, replica_groups=mesh['leaf'=4,'blk'=8] {'blk'}, use_global_device_ids=true, to_apply=%region_3.0.clone | all-reduce | flops 1536 | bytes 12288
  271.7 22.3 %all-reduce.2 = f32[1536]{0:T(1024)S(1)} all-reduce(f32[1536]{0:T(1024)S(1)} %dynamic-update-slice.72), channel_id=1, replica_groups=mesh['leaf'=4,'blk'=8] {'blk'}, use_global_device_ids=true, to_apply=%add.2 | all-reduce | flops 1536 | bytes 12288
  294.1 105.7 %all-gather.5.cloned.1.call-done = f32[1536,1536]{1,0:T(8,128)} async-done(((f32[192,1536]{1,0:T(8,128)}), f32[1536,1536]{1,0:T(8,128)}) %all-gather.5.cloned.1.call-update) | async-done | bytes 9437200 | tf_op jit(solution)/shard_map/all_gather | solution.py:48
  409.5 12.2 %add.225 = f32[1536,1536]{0,1:T(8,128)} add(f32[1536,1536]{0,1:T(8,128)} %copy.15, f32[1536,1536]{0,1:T(8,128)} %copy.16) | non-fusion elementwise | flops 2359296 | bytes 28311552 | tf_op jit(solution)/shard_map/add | solution.py:51
  431.5 12.2 %fusion = f32[1536,1536]{1,0:T(8,128)} fusion(f32[1536,1536]{1,0:T(8,128)} %copy.17, f32[1536,1536]{0,1:T(8,128)} %add.225), kind=kLoop, calls=%fused_computation.9 | loop fusion | flops 4718592 | bytes 28311552 | tf_op jit(solution)/shard_map/jit(cholesky)/div | solution.py:53
  444.5 11.7 %cholesky.340 = f32[128,128]{1,0:T(8,128)S(1)} custom-call(f32[128,128]{1,0:T(8,128)S(1)} %cholesky.889), custom_call_target="Cholesky" | custom-call | tf_op jit(solution)/shard_map/jit(cholesky)/cholesky | solution.py:53
  475.6 11.9 %cholesky.361 = f32[128,128]{1,0:T(8,128)S(1)} custom-call(f32[128,128]{1,0:T(8,128)S(1)} %cholesky.893), custom_call_target="Cholesky" | custom-call | tf_op jit(solution)/shard_map/jit(cholesky)/cholesky | solution.py:53
  502.3 11.7 %cholesky.384 = f32[128,128]{1,0:T(8,128)S(1)} custom-call(f32[128,128]{1,0:T(8,128)S(1)} %cholesky.898), custom_call_target="Cholesky" | custom-call | tf_op jit(solution)/shard_map/jit(cholesky)/cholesky | solution.py:53
  515.4 10.2 %custom-call.100 = f32[1,128,128]{1,2,0:T(8,128)S(1)} custom-call(f32[1,128,128]{2,1,0:T(8,128)S(1)} %get-tuple-element.192), custom_call_target="InvertDiagBlocksLowerTriangular" | custom-call | tf_op jit(solution)/shard_map/jit(cholesky)/cholesky | solution.py:53
  530.4 11.7 %cholesky.713 = f32[128,128]{1,0:T(8,128)S(1)} custom-call(f32[128,128]{1,0:T(8,128)S(1)} %cholesky.903), custom_call_target="Cholesky" | custom-call | tf_op jit(solution)/shard_map/jit(cholesky)/cholesky | solution.py:53
  558.3 11.9 %cholesky.732 = f32[128,128]{1,0:T(8,128)S(1)} custom-call(f32[128,128]{1,0:T(8,128)S(1)} %cholesky.908), custom_call_target="Cholesky" | custom-call | tf_op jit(solution)/shard_map/jit(cholesky)/cholesky | solution.py:53
  586.4 11.7 %cholesky.752 = f32[128,128]{1,0:T(8,128)S(1)} custom-call(f32[128,128]{1,0:T(8,128)S(1)} %cholesky.913), custom_call_target="Cholesky" | custom-call | tf_op jit(solution)/shard_map/jit(cholesky)/cholesky | solution.py:53
  599.4 10.0 %custom-call.103 = f32[1,128,128]{1,2,0:T(8,128)S(1)} custom-call(f32[1,128,128]{2,1,0:T(8,128)S(1)} %get-tuple-element.183), custom_call_target="InvertDiagBlocksLowerTriangular" | custom-call | tf_op jit(solution)/shard_map/jit(cholesky)/cholesky | solution.py:53
  614.5 11.7 %cholesky.772 = f32[128,128]{1,0:T(8,128)S(1)} custom-call(f32[128,128]{1,0:T(8,128)S(1)} %cholesky.918), custom_call_target="Cholesky" | custom-call | tf_op jit(solution)/shard_map/jit(cholesky)/cholesky | solution.py:53
  642.8 11.7 %cholesky.792 = f32[128,128]{1,0:T(8,128)S(1)} custom-call(f32[128,128]{1,0:T(8,128)S(1)} %cholesky.923), custom_call_target="Cholesky" | custom-call | tf_op jit(solution)/shard_map/jit(cholesky)/cholesky | solution.py:53
  670.3 11.8 %cholesky.812 = f32[128,128]{1,0:T(8,128)S(1)} custom-call(f32[128,128]{1,0:T(8,128)S(1)} %cholesky.928), custom_call_target="Cholesky" | custom-call | tf_op jit(solution)/shard_map/jit(cholesky)/cholesky | solution.py:53
  697.7 11.7 %cholesky.832 = f32[128,128]{1,0:T(8,128)S(1)} custom-call(f32[128,128]{1,0:T(8,128)S(1)} %cholesky.933), custom_call_target="Cholesky" | custom-call | tf_op jit(solution)/shard_map/jit(cholesky)/cholesky | solution.py:53
  724.2 11.9 %cholesky.852 = f32[128,128]{1,0:T(8,128)S(1)} custom-call(f32[128,128]{1,0:T(8,128)S(1)} %cholesky.938), custom_call_target="Cholesky" | custom-call | tf_op jit(solution)/shard_map/jit(cholesky)/cholesky | solution.py:53
  750.4 11.7 %cholesky.870 = f32[128,128]{1,0:T(8,128)S(1)} custom-call(f32[128,128]{1,0:T(8,128)S(1)} %convolution_subtract_fusion.3), custom_call_target="Cholesky" | custom-call | tf_op jit(solution)/shard_map/jit(cholesky)/cholesky | solution.py:53
  780.1 35.1 %while.19 = (s32[]{:T(128)}, f32[1536,1536]{1,0:T(8,128)}, s32[12,2]{0,1:T(2,128)S(1)}, f32[12,128,128]{2,1,0:T(8,128)S(1)}, s32[]{:T(128)}) while((s32[]{:T(128)}, f32[1536,1536]{1,0:T(8,128)}, s32[12,2]{0,1:T(2,128)S(1)}, f32[12,128,128]{2,1,0:T(8,128)S(1)}, s32[]{:T(128)}) %tuple.145), condition=%wide.while_cond, body=%wide.while_body.sunk | while | flops 2 | bytes 131181 | solution.py:54
  815.2 118.1 %custom-call.109 = f32[12,128,128]{1,2,0:T(8,128)S(1)} custom-call(f32[12,128,128]{2,1,0:T(8,128)S(1)} %get-tuple-element.144), custom_call_target="InvertDiagBlocksLowerTriangular" | custom-call | tf_op jit(solution)/shard_map/jit(_cho_solve)/triangular_solve | solution.py:54
  (283 shorter events, 303.4 us)
Async XLA Ops:
  7.2 3.0 copy-start
  7.2 208.1 %reduce-scatter.2.cloned.1.call-start = ((), (), s32[]{:S(2)}) async-start(), calls=%async_computation.1 | async-start | bytes 10616832 | tf_op jit(solution)/shard_map/reduce_scatter | solution.py:43
  49.2 166.2 %copy-start.4 = (f32[1,256]{1,0:T(1,128)S(1)}, f32[1,256]{1,0:T(1,128)}, u32[]{:S(2)}) copy-start(f32[1,256]{1,0:T(1,128)} %param.13) | copy-start | bytes 3076
  49.2 166.7 %copy-start.6 = (s32[1,64]{1,0:T(1,128)S(1)}, s32[1,64]{1,0:T(1,128)}, u32[]{:S(2)}) copy-start(s32[1,64]{1,0:T(1,128)} %param.11) | copy-start | bytes 772
  49.2 167.7 %copy-start.7 = (u32[32]{0:T(128)S(1)}, u32[32]{0:T(128)}, u32[]{:S(2)}) copy-start(u32[32]{0:T(128)} %constant.516) | copy-start | bytes 388
  49.2 168.3 %copy-start.5 = (u32[32]{0:T(128)S(1)}, u32[32]{0:T(128)}, u32[]{:S(2)}) copy-start(u32[32]{0:T(128)} %constant.521) | copy-start | bytes 388
  49.2 204.4 %all-gather.7.cloned.1.call-start = ((), (), s32[]{:S(2)}) async-start(), calls=%async_computation.3 | async-start | bytes 5898240 | tf_op jit(solution)/shard_map/all_gather | solution.py:8
  215.3 184.4 %all-gather.5.cloned.1.call-start = ((), (), s32[]{:S(2)}) async-start(), calls=%async_computation.2 | async-start | bytes 10616832 | tf_op jit(solution)/shard_map/all_gather | solution.py:48
  259.8 1.0 copy-start.1
  260.9 33.1 %copy-start.3 = (f32[1536]{0:T(1024)S(1)}, f32[1536]{0:T(1024)}, u32[]{:S(2)}) copy-start(f32[1536]{0:T(1024)} %param.14) | copy-start | bytes 18436
  780.1 190.0 %copy-start.2 = (f32[1,64,256]{2,1,0:T(8,128)S(1)}, f32[1,64,256]{2,1,0:T(8,128)}, u32[]{:S(2)}) copy-start(f32[1,64,256]{2,1,0:T(8,128)} %param.10) | copy-start | bytes 196612
Sparse Core Ops, SparseCore 0:
  49.3 165.9 reduce-scatter.1
  216.9 36.6 all-gather.6
  261.0 138.7 all-gather.4
where the time goes:
time: 989 us; the launch traced here: 979 us
  other arithmetic  450 us (46%)
  waiting for transfers between devices  280 us (28%)
  matrix products  88.5 us (9%)
  local copies, waits for them, and re-layouts  87.5 us (9%)
  blocking collectives  48.2 us (5%)
  between operations  25 us (3%)
    another operation x46, other arithmetic, shards(): lower_factor = jnp.linalg.cholesky(schur_matrix)  264 us
    reduce_scatter x1, waiting for transfers between devices, shards(): lax.psum_scatter(dense_term, 'blk', scatter_dimension=0, tiled=True)  166 us
    another operation x4, other arithmetic, shards(): solution = jax.scipy.linalg.cho_solve((lower_factor, True), iface_rhs)  127 us
    all_gather x1, waiting for transfers between devices, shards(): lax.all_gather(share_rows, 'blk', axis=0, tiled=True)  106 us
    another operation x22, matrix products, shards(): lower_factor = jnp.linalg.cholesky(schur_matrix)  50.3 us
    unnamed x3, blocking collectives  48.2 us
    another operation x36, local copies, waits for them, and re-layouts  34.9 us
    another operation x46, matrix products, shards(): solution = jax.scipy.linalg.cho_solve((lower_factor, True), iface_rhs)  34.9 us
  transfers between devices with their start and end apart: 3, of which 3 were waited for; matrix products, arithmetic and copies ran while one was open for 1% of the time, Pallas kernels for 0%

commit v1 on v0

v1 whole, which is shorter than its diff:
```python
import functools
import jax
import jax.numpy as jnp
from jax import lax
from jax.experimental import pallas as pl
from jax.experimental.pallas import tpu as pltpu
from jax.sharding import PartitionSpec as P

F32 = jnp.float32
BF16 = jnp.bfloat16
HIGHEST = lax.Precision.HIGHEST
NB = 128
TB = 256
NT = (((1,), (1,)), ((), ()))


def lane_of(x, j):
    return jnp.broadcast_to(x[:, j : j + 1], (8, 128))


def row_of(x, i):
    return jnp.broadcast_to(x[i : i + 1, :], (8, 128))


def split(x):
    high = x.astype(BF16)
    return high, (x - high.astype(F32)).astype(BF16)


def first_factors(x):
    high, low = split(x)
    return jnp.concatenate([high, high, low], axis=1)


def second_factors(x):
    high, low = split(x)
    return jnp.concatenate([high, low, high], axis=1)


def product(a, b):
    return lax.dot_general(a, b, NT, preferred_element_type=F32)


def inverse_root(T):
    T = list(T)
    groups = len(T)
    lane = lax.broadcasted_iota(jnp.int32, (8, 128), 1)
    sub = lax.broadcasted_iota(jnp.int32, (8, 128), 0)
    zero = jnp.zeros((8, 128), F32)
    W = [None] * groups

    def corner(columns):
        return [[row_of(columns[j], i) if i >= j else None for j in range(8)] for i in range(8)]

    G = corner([lane_of(T[0], j) for j in range(8)])
    after = [lane_of(T[1], j) for j in range(8)]
    ahead = [lane_of(T[1], 8 + j) for j in range(8)]
    for g in range(groups):
        last = g == groups - 1
        inside = (lane >= 8 * g) & (lane < 8 * g + 8)
        t = [jnp.where(inside, jnp.where(lane == 8 * g + j, 1.0, 0.0), row_of(T[g], j)) for j in range(8)]
        r = [None] * 8
        f = [[None] * 8 for _ in range(8)]
        if not last:
            following = jnp.where(inside, zero, T[g + 1])
        for p in range(8):
            r[p] = 1.0 / G[p][p]
            for j in range(p + 1, 8):
                f[j][p] = G[j][p] * r[p]
            for j in range(p + 1, 8):
                for k in range(p + 1, j + 1):
                    G[j][k] = G[j][k] - f[j][p] * G[k][p]
            for j in range(p + 1, 8):
                t[j] = t[j] - f[j][p] * t[p]
            if not last:
                scaled = after[p] * r[p]
                for j in range(8):
                    ahead[j] = ahead[j] - scaled * row_of(after[p], j)
                for k in range(p + 1, 8):
                    after[k] = after[k] - scaled * G[k][p]
                following = following - scaled * t[p]
        w = zero
        for p in range(8):
            w = jnp.where(sub == p, t[p] * jnp.sqrt(r[p]), w)
        W[g] = jnp.where(lane < 8 * g + 8, w, 0.0)
        if last:
            break
        T[g + 1] = following
        G = corner(ahead)
        if g + 2 < groups:
            e = [None] * 8
            for p in reversed(range(8)):
                e[p] = t[p] * r[p]
                for k in range(p + 1, 8):
                    e[p] = e[p] - f[k][p] * e[k]
            for i in range(g + 2, groups):
                old = T[i]
                T[i] = jnp.where(inside, zero, old)
                for j in range(8):
                    T[i] = T[i] - lane_of(old, 8 * g + j) * e[j]
            after = [lane_of(T[g + 2], 8 * (g + 1) + j) for j in range(8)]
            ahead = [lane_of(T[g + 2], 8 * (g + 2) + j) for j in range(8)]
    return W


def piece_kernel(count_ref, coupling_ref, factor_ref, resid_ref, rows_ref, out_ref):
    capacity, interior = coupling_ref.shape
    active = lax.broadcasted_iota(jnp.int32, (capacity, interior), 0) < count_ref[0]
    coupled = jnp.where(active, coupling_ref[...], 0.0)
    extra = jnp.broadcast_to(resid_ref[...], (8, interior))
    both = jnp.concatenate([coupled, extra], axis=0)
    reduced = lax.dot_general(both, factor_ref[...], NT, precision=HIGHEST, preferred_element_type=F32)
    square = lax.dot_general(reduced, reduced[:capacity], NT, precision=HIGHEST, preferred_element_type=F32)
    half = capacity // 2
    out_ref[0:half, 0:capacity] = square[0:half]
    out_ref[0:half, capacity : 2 * capacity] = square[half:capacity]
    out_ref[half : half + 8, 0:capacity] = square[capacity : capacity + 8]
    out_ref[half : half + 8, capacity : 2 * capacity] = jnp.broadcast_to(
        rows_ref[...].astype(F32), (8, capacity)
    )


def system_kernel(
    steps,
    n,
    me_ref,
    own_rows_ref,
    count_ref,
    pieces_ref,
    operator_ref,
    resid_iface_ref,
    coupling_ref,
    factor_ref,
    resid_ref,
    interior_ref,
    iface_ref,
    M,
    by_row,
    z_rows,
    listed,
    listed_int,
    inverse,
    rhs,
    first,
    second,
    roots,
    x_columns,
    picked,
    listed_smem,
    sem_operator,
    sem_listed,
):
    S = M.shape[0]
    chunks = S // 128
    capacity = coupling_ref.shape[0]
    half = capacity // 2
    size = half + 8
    me = me_ref[0]
    lane = lax.broadcasted_iota(jnp.int32, (8, 128), 1)
    sub = lax.broadcasted_iota(jnp.int32, (8, 128), 0)

    get_operator = pltpu.make_async_copy(operator_ref, M, sem_operator)
    get_operator.start()

    def slot_of(k):
        bits = k ^ me
        slot = 0
        for t, bit in enumerate(steps):
            slot = slot + (((bits >> bit) & 1) << t)
        return slot

    def list_rows(k, carry):
        listed[pl.ds(k, 1), :] = pieces_ref[pl.ds(slot_of(k) * size + half, 1), :]
        return carry

    lax.fori_loop(0, n, list_rows, 0)
    listed_int[...] = listed[...].astype(jnp.int32)
    get_listed = pltpu.make_async_copy(listed_int, listed_smem, sem_listed)
    get_listed.start()

    def clear(i, carry):
        by_row[pl.ds(pl.multiple_of(i * 128, 128), 128), :] = jnp.zeros((128, 128), F32)
        return carry

    lax.fori_loop(0, by_row.shape[0] // 128, clear, 0)

    def invert(b, carry):
        rows8 = listed_int[pl.ds(pl.multiple_of(b * 8, 8), 8), :]
        found = [jnp.full((8, 128), -1, jnp.int32) for _ in range(chunks)]
        for i in range(capacity):
            target = lane_of(rows8, capacity + i)
            for c in range(chunks):
                found[c] = jnp.where(lane + 128 * c == target, i, found[c])
        for c in range(chunks):
            inverse[pl.ds(pl.multiple_of(c * n + b * 8, 8), 8), :] = found[c]
        return carry

    lax.fori_loop(0, n // 8, invert, 0)
    get_listed.wait()

    rhs[...] = jnp.broadcast_to(resid_iface_ref[...], rhs.shape)

    def scatter(k, carry):
        base = slot_of(k) * size
        strips = [pieces_ref[pl.ds(pl.multiple_of(base + 8 * s, 8), 8), :] for s in range(size // 8)]
        for c in range(chunks):
            at = jnp.broadcast_to(inverse[pl.ds(c * n + k, 1), :], (8, 128))
            member = at >= 0
            low = jnp.maximum(at, 0)
            high = low + capacity
            for s in range(half // 8):
                for which, index in ((0, low), (half, high)):
                    spread = jnp.take_along_axis(strips[s], index, axis=1, mode="promise_in_bounds")
                    z_rows[pl.ds((which + 8 * s) * 16 + c, 8, stride=16), :] = jnp.where(member, spread, 0.0)
            spread = jnp.take_along_axis(strips[half // 8], low, axis=1, mode="promise_in_bounds")
            spread = jnp.where(member, spread, 0.0)
            cols = slice(128 * c, 128 * (c + 1))
            rhs[0:8, cols] = rhs[0:8, cols] + spread
        for i in range(0, capacity, 8):
            places = [pl.multiple_of(listed_smem[k, capacity + i + u] * 16, 16) for u in range(8)]
            sums = [
                by_row[pl.ds(places[u], 16), :] + z_rows[16 * (i + u) : 16 * (i + u + 1), :] for u in range(8)
            ]
            for u in range(8):
                by_row[pl.ds(places[u], 16), :] = sums[u]
        return carry

    lax.fori_loop(0, n, scatter, 0)
    rhs[8:16, :] = rhs[0:8, :]
    get_operator.wait()

    def assemble(q, carry):
        row = pl.multiple_of(q * 8, 8)
        for c in range(chunks):
            cols = slice(128 * c, 128 * (c + 1))
            M[pl.ds(row, 8), cols] = M[pl.ds(row, 8), cols] + by_row[pl.ds(row * 16 + c, 8, stride=16), :]
        return carry

    lax.fori_loop(0, S // 8, assemble, 0)

    panels = S // NB
    tiles = S // TB

    def panel(j, carry):
        at = pl.multiple_of(j * NB, NB)
        here = pl.ds(at, NB)
        W = inverse_root([M[pl.ds(at + 8 * s, 8), here] for s in range(NB // 8)])
        W = jnp.concatenate(W, axis=0)
        roots[here, :] = W.T
        W_second = second_factors(W)
        z = product(first_factors(rhs[:, here]), W_second)
        rhs[:, here] = z
        z_first = first_factors(z)
        first[here, :] = jnp.zeros((NB, 3 * NB), BF16)
        second[here, :] = jnp.zeros((NB, 3 * NB), BF16)

        def column(i, carry):
            rows = pl.ds(pl.multiple_of(i * NB, NB), NB)
            V = product(first_factors(M[rows, here]), W_second)
            M[rows, here] = V
            first[rows, :] = first_factors(V)
            second[rows, :] = second_factors(V)
            return carry

        lax.fori_loop(j + 1, panels, column, 0)

        def across(b, carry):
            cols = pl.ds(pl.multiple_of(b * TB, TB), TB)
            weights = second[cols, :]
            rhs[:, cols] = rhs[:, cols] - product(z_first, weights)

            def down(a, carry):
                rows = pl.ds(pl.multiple_of(a * TB, TB), TB)
                M[rows, cols] = M[rows, cols] - product(first[rows, :], weights)
                return carry

            lax.fori_loop(b, tiles, down, 0)
            return carry

        @pl.when(j + 1 < panels)
        def _():
            lax.fori_loop((j + 1) // 2, tiles, across, 0)

        return carry

    lax.fori_loop(0, panels, panel, 0)

    def back(step, carry):
        j = panels - 1 - step
        at = pl.multiple_of(j * NB, NB)
        t = jnp.broadcast_to(rhs[0:1, pl.ds(at, NB)], (8, NB))
        x = []
        flat = jnp.zeros((8, 128), F32)
        for s in range(NB // 8):
            total = jnp.sum(roots[pl.ds(at + 8 * s, 8), :] * t, axis=1, keepdims=True)
            total = jnp.broadcast_to(total, (8, 128))
            x.append(total)
            x_columns[pl.ds(at + 8 * s, 8), :] = total
            flat = flat + jnp.where(lane == sub + 8 * s, total, 0.0)
        iface_ref[:, pl.ds(at, NB)] = jnp.sum(flat, axis=0, keepdims=True)
        for c in range(chunks):
            cols = slice(128 * c, 128 * (c + 1))
            total = x[0] * M[pl.ds(at, 8), cols]
            for s in range(1, NB // 8):
                total = total + x[s] * M[pl.ds(at + 8 * s, 8), cols]
            rhs[0:1, cols] = rhs[0:1, cols] - jnp.sum(total, axis=0, keepdims=True)
        return carry

    lax.fori_loop(0, panels, back, 0)

    for i in range(capacity):
        picked[i : i + 1, :] = x_columns[pl.ds(own_rows_ref[0, i], 1), :]
    interior = coupling_ref.shape[1]
    corrected = []
    for c in range(interior // 128):
        cols = slice(128 * c, 128 * (c + 1))
        row = lax.broadcasted_iota(jnp.int32, (capacity, 128), 0)
        terms = jnp.where(row < count_ref[0], coupling_ref[:, cols] * picked[...], 0.0)
        corrected.append(resid_ref[:, cols] - jnp.sum(terms, axis=0, keepdims=True))
    corrected = jnp.concatenate(corrected, axis=1)
    inner = jnp.sum(factor_ref[...] * corrected, axis=1, keepdims=True)
    interior_ref[...] = jnp.sum(factor_ref[...] * inner, axis=0, keepdims=True)


def shards(leaf, blk, interior_factor, coupling, iface_rows, counts, resid_interior, resid_iface, iface_operator):
    factor = interior_factor[0]
    couple = coupling[0]
    capacity, interior = couple.shape
    S = iface_operator.shape[0]
    n = leaf * blk
    vmem = pl.BlockSpec(memory_space=pltpu.VMEM)
    smem = pl.BlockSpec(memory_space=pltpu.SMEM)
    anywhere = pl.BlockSpec(memory_space=pl.ANY)
    size = capacity // 2 + 8

    gathered = pl.pallas_call(
        piece_kernel,
        out_shape=jax.ShapeDtypeStruct((size, 2 * capacity), F32),
        in_specs=[smem, vmem, vmem, vmem, vmem],
        out_specs=vmem,
    )(counts, couple, factor, resid_interior, iface_rows)

    steps = []
    for axis, width, low in (("blk", blk, 0), ("leaf", leaf, blk.bit_length() - 1)):
        for bit in reversed(range(width.bit_length() - 1)):
            other = lax.ppermute(gathered, axis, [(i, i ^ (1 << bit)) for i in range(width)])
            gathered = jnp.concatenate([gathered, other], axis=0)
            steps.append(low + bit)

    me = (lax.axis_index("leaf") * blk + lax.axis_index("blk")).astype(jnp.int32).reshape(1)
    interior_out, iface = pl.pallas_call(
        functools.partial(system_kernel, tuple(steps), n),
        out_shape=(
            jax.ShapeDtypeStruct((1, interior), F32),
            jax.ShapeDtypeStruct((1, S), F32),
        ),
        in_specs=[smem, smem, smem, vmem, anywhere, vmem, vmem, vmem, vmem],
        out_specs=(vmem, vmem),
        scratch_shapes=[
            pltpu.VMEM((S, S), F32),
            pltpu.VMEM((S * 16, 128), F32),
            pltpu.VMEM((capacity * 16, 128), F32),
            pltpu.VMEM((n, 128), F32),
            pltpu.VMEM((n, 128), jnp.int32),
            pltpu.VMEM((n * S // 128, 128), jnp.int32),
            pltpu.VMEM((16, S), F32),
            pltpu.VMEM((S, 3 * NB), BF16),
            pltpu.VMEM((S, 3 * NB), BF16),
            pltpu.VMEM((S, NB), F32),
            pltpu.VMEM((S, 128), F32),
            pltpu.VMEM((capacity, 128), F32),
            pltpu.SMEM((n, 128), jnp.int32),
            pltpu.SemaphoreType.DMA,
            pltpu.SemaphoreType.DMA,
        ],
        compiler_params=pltpu.CompilerParams(vmem_limit_bytes=48 * 1024 * 1024),
    )(
        me,
        iface_rows,
        counts,
        gathered,
        iface_operator,
        resid_iface.reshape(1, S),
        couple,
        factor,
        resid_interior,
    )
    own = S // blk
    own_part = lax.dynamic_slice_in_dim(iface[0], lax.axis_index("blk") * own, own, 0)
    return interior_out, own_part


def solution(mesh):
    spec = ("leaf", "blk")
    return jax.shard_map(
        functools.partial(shards, mesh.shape["leaf"], mesh.shape["blk"]),
        mesh=mesh,
        in_specs=(
            P(spec, None, None),
            P(spec, None, None),
            P(spec, None),
            P(spec),
            P(spec, None),
            P(),
            P(),
        ),
        out_specs=(P(spec, None), P("blk")),
        check_vma=False,
    )
```

time: 989 us -> 135 us (0.14)
  other arithmetic: 450 us -> 2.21 us
  waiting for transfers between devices: 280 us -> 10.1 us
  Pallas kernels: 0 us -> 105 us
  matrix products: 88.5 us -> 0 us
  local copies, waits for them, and re-layouts: 87.5 us -> 5.26 us
  blocking collectives: 48.2 us -> 0 us
  between operations: 25 us -> 1.33 us
    another operation x50 -> x0, other arithmetic: 391 us -> none  [the longest x46 264 us: shards(): lower_factor = jnp.linalg.cholesky(schur_matrix)]
    reduce_scatter x1 -> x0, waiting for transfers between devices: 166 us -> none  [shards(): lax.psum_scatter(dense_term, 'blk', scatter_dimension=0, tiled=True)]
    all_gather x2 -> x0, waiting for transfers between devices: 114 us -> none  [the longest x1 106 us: shards(): lax.all_gather(share_rows, 'blk', axis=0, tiled=True)]
    pallas_call x0 -> x2, Pallas kernels: none -> 105 us  [the longest x1 103 us: shards(): pl.pallas_call(functools.partial(system_kernel, tuple(steps), n), out_sha...]
    another operation x68 -> x0, matrix products: 85.2 us -> none  [the longest x22 50.3 us: shards(): lower_factor = jnp.linalg.cholesky(schur_matrix)]
    unnamed x3 -> x0, blocking collectives: 48.2 us -> none
    another operation x57 -> x0, local copies, waits for them, and re-layouts: 40.7 us -> none
    unnamed x5 -> x0, other arithmetic: 27.3 us -> none
  transfers between devices with their start and end apart: 3 -> 5, of which waited for: 3 -> 5; matrix products, arithmetic and copies ran while one was open for 1% -> 1% of each run, Pallas kernels for 0% -> 0%
where the time goes in v1:
time: 135 us; the launch traced here: 134 us
  Pallas kernels  105 us (78%)
  waiting for transfers between devices  10.1 us (7%)
  starting transfers between devices  9.92 us (7%)
  local copies, waits for them, and re-layouts  5.26 us (4%)
  other arithmetic  2.21 us (2%)
    pallas_call x1, Pallas kernels, shards(): pl.pallas_call(functools.partial(system_kernel, tuple(steps), n), out_sha...  103 us
    ppermute x5, waiting for transfers between devices, shards(): lax.ppermute(gathered, axis, [(i, i ^ 1 << bit) for i in range(width)])  10.1 us
    ppermute x5, starting transfers between devices, shards(): lax.ppermute(gathered, axis, [(i, i ^ 1 << bit) for i in range(width)])  9.92 us
    unnamed x12, local copies, waits for them, and re-layouts  3.87 us
  transfers between devices with their start and end apart: 5, of which 5 were waited for; matrix products, arithmetic and copies ran while one was open for 1% of the time, Pallas kernels for 0%

profile of v1, /device:TPU:0, one launch (start us, length us, event | category | flops | bytes accessed | tf_op | source)
XLA Modules:
  0.0 134.3 jit_solution(13469284908635883709)
XLA Ops:
  1.3 2.3 %shard_map.86 = f32[40,128]{1,0:T(8,128)} custom-call(s32[1]{0:T(128)S(6)} %copy.18.count_ref, f32[64,256]{1,0:T(8,128)} %bitcast.6, f32[256,256]{1,0:T(8,128)} %bitcast.4, f32[1,256]{1,0:T(1,128)} %resid_ref.3, s32[1,64]{1,0:T(1,128)} %own_rows_ref.1), custom_call_target="tpu_custom_call" | custom-call | tf_op jit(solution)/shard_map/pallas_call | solution.py:336
  3.5 4.0 %collective-permute-start = (f32[40,128]{1,0:T(8,128)}, f32[40,128]{1,0:T(8,128)S(1)}, u32[]{:S(2)}, u32[]{:S(2)}) collective-permute-start(f32[40,128]{1,0:T(8,128)} %shard_map.86), channel_id=1, source_target_pairs={{0,4},{1,5},{2,6},{3,7},{4,0},{5,1},{6,2},{7,3},{8,12},{9,13},{10,... | collective-permute-start | bytes 61448 | tf_op jit(solution)/shard_map/ppermute | solution.py:346
  7.6 2.0 %collective-permute-done = f32[40,128]{1,0:T(8,128)S(1)} collective-permute-done((f32[40,128]{1,0:T(8,128)}, f32[40,128]{1,0:T(8,128)S(1)}, u32[]{:S(2)}, u32[]{:S(2)}) %collective-permute-start) | collective-permute-done | bytes 20512 | tf_op jit(solution)/shard_map/ppermute | solution.py:346
  9.6 0.7 pad_maximum_fusion.2
  10.3 1.9 %collective-permute-start.1 = (f32[80,128]{1,0:T(8,128)S(1)}, f32[80,128]{1,0:T(8,128)S(1)}, u32[]{:S(2)}, u32[]{:S(2)}) collective-permute-start(f32[80,128]{1,0:T(8,128)S(1)} %pad_maximum_fusion.2), channel_id=1, source_target_pairs={{0,2},{1,3},{2,0},{3,1},{4,6},{5,7},{6,4},{7,5},{8,10},{9,11},{10,... | collective-permute-start | bytes 122888 | tf_op jit(solution)/shard_map/ppermute | solution.py:346
  12.2 0.7 constant_dynamic-update-slice_fusion.4
  12.9 1.4 %collective-permute-done.1 = f32[80,128]{1,0:T(8,128)S(1)} collective-permute-done((f32[80,128]{1,0:T(8,128)S(1)}, f32[80,128]{1,0:T(8,128)S(1)}, u32[]{:S(2)}, u32[]{:S(2)}) %collective-permute-start.1) | collective-permute-done | bytes 40992 | tf_op jit(solution)/shard_map/ppermute | solution.py:346
  14.3 0.7 pad_maximum_fusion.1
  15.0 1.9 %collective-permute-start.2 = (f32[160,128]{1,0:T(8,128)S(1)}, f32[160,128]{1,0:T(8,128)S(1)}, u32[]{:S(2)}, u32[]{:S(2)}) collective-permute-start(f32[160,128]{1,0:T(8,128)S(1)} %pad_maximum_fusion.1), channel_id=1, source_target_pairs={{0,1},{1,0},{2,3},{3,2},{4,5},{5,4},{6,7},{7,6},{8,9},{9,8},{10,11... | collective-permute-start | bytes 245768 | tf_op jit(solution)/shard_map/ppermute | solution.py:346
  17.0 2.5 %collective-permute-done.2 = f32[160,128]{1,0:T(8,128)S(1)} collective-permute-done((f32[160,128]{1,0:T(8,128)S(1)}, f32[160,128]{1,0:T(8,128)S(1)}, u32[]{:S(2)}, u32[]{:S(2)}) %collective-permute-start.2) | collective-permute-done | bytes 81952 | tf_op jit(solution)/shard_map/ppermute | solution.py:346
  19.5 0.7 pad_maximum_fusion
  20.2 2.0 %collective-permute-start.3 = (f32[320,128]{1,0:T(8,128)S(1)}, f32[320,128]{1,0:T(8,128)S(1)}, u32[]{:S(2)}, u32[]{:S(2)}) collective-permute-start(f32[320,128]{1,0:T(8,128)S(1)} %pad_maximum_fusion), channel_id=1, source_target_pairs={{0,16},{8,24},{16,0},{24,8},{1,17},{9,25},{17,1},{25,9},{2,18},{10... | collective-permute-start | bytes 491528 | tf_op jit(solution)/shard_map/ppermute | solution.py:346
  22.2 3.4 %collective-permute-done.3 = f32[320,128]{1,0:T(8,128)S(1)} collective-permute-done((f32[320,128]{1,0:T(8,128)S(1)}, f32[320,128]{1,0:T(8,128)S(1)}, u32[]{:S(2)}, u32[]{:S(2)}) %collective-permute-start.3) | collective-permute-done | bytes 163872 | tf_op jit(solution)/shard_map/ppermute | solution.py:346
  25.6 0.1 collective-permute-start.4
  25.7 0.7 reshape.12.resid_iface_ref
  26.4 0.9 collective-permute-done.4
  27.3 0.0 copy-start
  27.4 0.9 copy-done
  28.3 0.0 copy-start.1
  28.3 0.8 copy-done.1
  29.1 0.7 copy-done.2
  29.8 0.7 copy-done.3
  30.5 103.1 %shard_map.87 = (f32[1,256]{1,0:T(1,128)}, f32[1,1536]{1,0:T(1,128)S(1)}) custom-call(s32[1]{0:T(128)} %bitcast.me_ref, s32[1,64]{1,0:T(1,128)S(1)} %copy-done.3, s32[1]{0:T(128)S(6)} %copy.18.count_ref, f32[1280,128]{1,0:T(8,128)S(1)} %constant_dynamic-update-slice_fusion.5.pieces_ref, f32[1536,1536]{1,0:T(8,128)} %operator_ref.1, ...), custom_call_target="tpu_custom_call" | custom-call | tf_op jit(solution)/shard_map/pallas_call | solution.py:351
  133.6 0.6 constant_dynamic-slice_fusion
  (7 shorter events, 0.1 us)
Async XLA Ops:
  3.5 6.0 %collective-permute-start = (f32[40,128]{1,0:T(8,128)}, f32[40,128]{1,0:T(8,128)S(1)}, u32[]{:S(2)}, u32[]{:S(2)}) collective-permute-start(f32[40,128]{1,0:T(8,128)} %shard_map.86), channel_id=1, source_target_pairs={{0,4},{1,5},{2,6},{3,7},{4,0},{5,1},{6,2},{7,3},{8,12},{9,13},{10,... | collective-permute-start | bytes 61448 | tf_op jit(solution)/shard_map/ppermute | solution.py:346
  10.3 4.0 %collective-permute-start.1 = (f32[80,128]{1,0:T(8,128)S(1)}, f32[80,128]{1,0:T(8,128)S(1)}, u32[]{:S(2)}, u32[]{:S(2)}) collective-permute-start(f32[80,128]{1,0:T(8,128)S(1)} %pad_maximum_fusion.2), channel_id=1, source_target_pairs={{0,2},{1,3},{2,0},{3,1},{4,6},{5,7},{6,4},{7,5},{8,10},{9,11},{10,... | collective-permute-start | bytes 122888 | tf_op jit(solution)/shard_map/ppermute | solution.py:346
  15.0 4.4 %collective-permute-start.2 = (f32[160,128]{1,0:T(8,128)S(1)}, f32[160,128]{1,0:T(8,128)S(1)}, u32[]{:S(2)}, u32[]{:S(2)}) collective-permute-start(f32[160,128]{1,0:T(8,128)S(1)} %pad_maximum_fusion.1), channel_id=1, source_target_pairs={{0,1},{1,0},{2,3},{3,2},{4,5},{5,4},{6,7},{7,6},{8,9},{9,8},{10,11... | collective-permute-start | bytes 245768 | tf_op jit(solution)/shard_map/ppermute | solution.py:346
  20.2 5.4 %collective-permute-start.3 = (f32[320,128]{1,0:T(8,128)S(1)}, f32[320,128]{1,0:T(8,128)S(1)}, u32[]{:S(2)}, u32[]{:S(2)}) collective-permute-start(f32[320,128]{1,0:T(8,128)S(1)} %pad_maximum_fusion), channel_id=1, source_target_pairs={{0,16},{8,24},{16,0},{24,8},{1,17},{9,25},{17,1},{25,9},{2,18},{10... | collective-permute-start | bytes 491528 | tf_op jit(solution)/shard_map/ppermute | solution.py:346
  25.6 1.7 %collective-permute-start.4 = (f32[640,128]{1,0:T(8,128)S(1)}, f32[640,128]{1,0:T(8,128)S(1)}, u32[]{:S(2)}, u32[]{:S(2)}) collective-permute-start(f32[640,128]{1,0:T(8,128)S(1)} %get-tuple-element.6), channel_id=1, source_target_pairs={{0,8},{8,0},{16,24},{24,16},{1,9},{9,1},{17,25},{25,17},{2,10},{10... | collective-permute-start | bytes 983048 | tf_op jit(solution)/shard_map/ppermute | solution.py:346
  27.3 1.0 copy-start
  28.3 0.8 copy-start.1
  29.1 0.7 copy-start.2
  29.8 0.7 copy-start.3

commit v2 on v1

--- a/solution.py
+++ b/solution.py
@@ -41,66 +41,58 @@
     return lax.dot_general(a, b, NT, preferred_element_type=F32)
 
 
-def inverse_root(T):
+def inverse_root(T, W):
     T = list(T)
     groups = len(T)
     lane = lax.broadcasted_iota(jnp.int32, (8, 128), 1)
     sub = lax.broadcasted_iota(jnp.int32, (8, 128), 0)
     zero = jnp.zeros((8, 128), F32)
-    W = [None] * groups
-
-    def corner(columns):
-        return [[row_of(columns[j], i) if i >= j else None for j in range(8)] for i in range(8)]
-
-    G = corner([lane_of(T[0], j) for j in range(8)])
+    is_row = [sub == p for p in range(8)]
+    own = [lane_of(T[0], j) for j in range(8)]
     after = [lane_of(T[1], j) for j in range(8)]
     ahead = [lane_of(T[1], 8 + j) for j in range(8)]
     for g in range(groups):
         last = g == groups - 1
         inside = (lane >= 8 * g) & (lane < 8 * g + 8)
-        t = [jnp.where(inside, jnp.where(lane == 8 * g + j, 1.0, 0.0), row_of(T[g], j)) for j in range(8)]
-        r = [None] * 8
-        f = [[None] * 8 for _ in range(8)]
+        t = jnp.where(inside, jnp.where(lane - 8 * g == sub, 1.0, 0.0), T[g])
+        w = zero
+        inverses = zero
         if not last:
             following = jnp.where(inside, zero, T[g + 1])
         for p in range(8):
-            r[p] = 1.0 / G[p][p]
-            for j in range(p + 1, 8):
-                f[j][p] = G[j][p] * r[p]
-            for j in range(p + 1, 8):
-                for k in range(p + 1, j + 1):
-                    G[j][k] = G[j][k] - f[j][p] * G[k][p]
-            for j in range(p + 1, 8):
-                t[j] = t[j] - f[j][p] * t[p]
+            pivot = row_of(own[p], p)
+            r = 1.0 / pivot
+            f = jnp.where(is_row[p], 0.0, own[p] * r)
+            across = [row_of(own[k], p) if k > p else None for k in range(8)]
+            u = row_of(t, p)
             if not last:
-                scaled = after[p] * r[p]
+                scaled = after[p] * r
                 for j in range(8):
                     ahead[j] = ahead[j] - scaled * row_of(after[p], j)
                 for k in range(p + 1, 8):
-                    after[k] = after[k] - scaled * G[k][p]
-                following = following - scaled * t[p]
-        w = zero
-        for p in range(8):
-            w = jnp.where(sub == p, t[p] * jnp.sqrt(r[p]), w)
-        W[g] = jnp.where(lane < 8 * g + 8, w, 0.0)
-        if last:
-            break
-        T[g + 1] = following
-        G = corner(ahead)
+                    after[k] = after[k] - scaled * across[k]
+                following = following - scaled * u
+            for k in range(p + 1, 8):
+                own[k] = own[k] - f * across[k]
+            w = jnp.where(is_row[p], u * lax.rsqrt(pivot), w)
+            t = t - f * u
+            inverses = jnp.where(is_row[p], r, inverses)
+        W.append(jnp.where(lane < 8 * g + 8, w, 0.0))
+        if not last:
+            T[g + 1] = following
+            own = ahead
         if g + 2 < groups:
-            e = [None] * 8
-            for p in reversed(range(8)):
-                e[p] = t[p] * r[p]
-                for k in range(p + 1, 8):
-                    e[p] = e[p] - f[k][p] * e[k]
+            E = t * inverses
+            e = [row_of(E, p) for p in range(8)]
             for i in range(g + 2, groups):
                 old = T[i]
-                T[i] = jnp.where(inside, zero, old)
-                for j in range(8):
-                    T[i] = T[i] - lane_of(old, 8 * g + j) * e[j]
+                terms = [lane_of(old, 8 * g + j) * e[j] for j in range(8)]
+                while len(terms) > 1:
+                    terms = [x + y for x, y in zip(terms[::2], terms[1::2])]
+                T[i] = jnp.where(inside, zero, old) - terms[0]
             after = [lane_of(T[g + 2], 8 * (g + 1) + j) for j in range(8)]
             ahead = [lane_of(T[g + 2], 8 * (g + 2) + j) for j in range(8)]
-    return W
+        yield
 
 
 def piece_kernel(count_ref, coupling_ref, factor_ref, resid_ref, rows_ref, out_ref):
@@ -239,51 +231,62 @@
     lax.fori_loop(0, S // 8, assemble, 0)
 
     panels = S // NB
-    tiles = S // TB
-
-    def panel(j, carry):
-        at = pl.multiple_of(j * NB, NB)
-        here = pl.ds(at, NB)
-        W = inverse_root([M[pl.ds(at + 8 * s, 8), here] for s in range(NB // 8)])
+
+    def block(i):
+        return slice(NB * i, NB * (i + 1))
+
+    def finish(p, W):
+        W_second = second_factors(W)
+        state = {}
+
+        def begin():
+            roots[block(p), :] = W.T
+            z = product(first_factors(rhs[:, block(p)]), W_second)
+            rhs[:, block(p)] = z
+            state["z"] = first_factors(z)
+
+        def column(i):
+            V = product(first_factors(M[block(i), block(p)]), W_second)
+            M[block(i), block(p)] = V
+            first[block(i), :] = first_factors(V)
+            second[block(i), :] = second_factors(V)
+
+        def right(cols):
+            rhs[:, cols] = rhs[:, cols] - product(state["z"], second[cols, :])
+
+        def tile(rows, cols):
+            M[rows, cols] = M[rows, cols] - product(first[rows, :], second[cols, :])
+
+        spans = [slice(at, min(at + TB, S)) for at in range(NB * (p + 1), S, TB)]
+        work = [begin]
+        work += [functools.partial(column, i) for i in range(p + 2, panels)]
+        for at, cols in enumerate(spans):
+            work.append(functools.partial(right, cols))
+            work += [functools.partial(tile, rows, cols) for rows in spans[at:]]
+        return work
+
+    work = []
+    D = M[block(0), block(0)]
+    for j in range(panels):
+        W = []
+        groups = NB // 8
+        done = 0
+        for g, _ in enumerate(inverse_root([D[8 * s : 8 * s + 8] for s in range(groups)], W)):
+            upto = len(work) * (g + 1) // groups
+            for item in work[done:upto]:
+                item()
+            done = upto
         W = jnp.concatenate(W, axis=0)
-        roots[here, :] = W.T
-        W_second = second_factors(W)
-        z = product(first_factors(rhs[:, here]), W_second)
-        rhs[:, here] = z
-        z_first = first_factors(z)
-        first[here, :] = jnp.zeros((NB, 3 * NB), BF16)
-        second[here, :] = jnp.zeros((NB, 3 * NB), BF16)
-
-        def column(i, carry):
-            rows = pl.ds(pl.multiple_of(i * NB, NB), NB)
-            V = product(first_factors(M[rows, here]), W_second)
-            M[rows, here] = V
-            first[rows, :] = first_factors(V)
-            second[rows, :] = second_factors(V)
-            return carry
-
-        lax.fori_loop(j + 1, panels, column, 0)
-
-        def across(b, carry):
-            cols = pl.ds(pl.multiple_of(b * TB, TB), TB)
-            weights = second[cols, :]
-            rhs[:, cols] = rhs[:, cols] - product(z_first, weights)
-
-            def down(a, carry):
-                rows = pl.ds(pl.multiple_of(a * TB, TB), TB)
-                M[rows, cols] = M[rows, cols] - product(first[rows, :], weights)
-                return carry
-
-            lax.fori_loop(b, tiles, down, 0)
-            return carry
-
-        @pl.when(j + 1 < panels)
-        def _():
-            lax.fori_loop((j + 1) // 2, tiles, across, 0)
-
-        return carry
-
-    lax.fori_loop(0, panels, panel, 0)
+        work = finish(j, W)
+        if j + 1 < panels:
+            V = product(first_factors(M[block(j + 1), block(j)]), second_factors(W))
+            M[block(j + 1), block(j)] = V
+            V_first, V_second = first_factors(V), second_factors(V)
+            first[block(j + 1), :] = V_first
+            second[block(j + 1), :] = V_second
+            D = M[block(j + 1), block(j + 1)] - product(V_first, V_second)
+    for item in work:
+        item()
 
     def back(step, carry):
         j = panels - 1 - step

time: 135 us -> 91.6 us (0.68)
  Pallas kernels: 105 us -> 62.2 us
    pallas_call x1, Pallas kernels: 103 us -> 60 us  [shards(): pl.pallas_call(functools.partial(system_kernel, tuple(steps), n), out_sha...]
  transfers between devices with their start and end apart: 5 -> 5, of which waited for: 5 -> 5; matrix products, arithmetic and copies ran while one was open for 1% -> 2% of each run, Pallas kernels for 0% -> 0%
where the time goes in v2:
time: 91.6 us; the launch traced here: 91.1 us
  Pallas kernels  62.2 us (68%)
  waiting for transfers between devices  10.1 us (11%)
  starting transfers between devices  9.92 us (11%)
  local copies, waits for them, and re-layouts  5.26 us (6%)
  other arithmetic  2.21 us (2%)
  between operations  1.33 us (1%)
    pallas_call x1, Pallas kernels, shards(): pl.pallas_call(functools.partial(system_kernel, tuple(steps), n), out_sha...  60 us
    ppermute x5, waiting for transfers between devices, shards(): lax.ppermute(gathered, axis, [(i, i ^ 1 << bit) for i in range(width)])  10.1 us
    ppermute x5, starting transfers between devices, shards(): lax.ppermute(gathered, axis, [(i, i ^ 1 << bit) for i in range(width)])  9.92 us
    unnamed x12, local copies, waits for them, and re-layouts  3.87 us
    pallas_call x1, Pallas kernels, shards(): pl.pallas_call(piece_kernel, out_shape=jax.ShapeDtypeStruct((size, 2 * ca...  2.27 us
    concatenate x3, other arithmetic, shards(): gathered = jnp.concatenate([gathered, other], axis=0)  2.21 us
  transfers between devices with their start and end apart: 5, of which 5 were waited for; matrix products, arithmetic and copies ran while one was open for 2% of the time, Pallas kernels for 0%

profile of v2, /device:TPU:0, one launch (start us, length us, event | category | flops | bytes accessed | tf_op | source)
XLA Modules:
  0.0 91.1 jit_solution(11474326644775634878)
XLA Ops:
  1.3 2.3 %shard_map.86 = f32[40,128]{1,0:T(8,128)} custom-call(s32[1]{0:T(128)S(6)} %copy.18.count_ref, f32[64,256]{1,0:T(8,128)} %bitcast.6, f32[256,256]{1,0:T(8,128)} %bitcast.4, f32[1,256]{1,0:T(1,128)} %resid_ref.3, s32[1,64]{1,0:T(1,128)} %own_rows_ref.1), custom_call_target="tpu_custom_call" | custom-call | tf_op jit(solution)/shard_map/pallas_call | solution.py:339
  3.5 4.0 %collective-permute-start = (f32[40,128]{1,0:T(8,128)}, f32[40,128]{1,0:T(8,128)S(1)}, u32[]{:S(2)}, u32[]{:S(2)}) collective-permute-start(f32[40,128]{1,0:T(8,128)} %shard_map.86), channel_id=1, source_target_pairs={{0,4},{1,5},{2,6},{3,7},{4,0},{5,1},{6,2},{7,3},{8,12},{9,13},{10,... | collective-permute-start | bytes 61448 | tf_op jit(solution)/shard_map/ppermute | solution.py:349
  7.6 2.0 %collective-permute-done = f32[40,128]{1,0:T(8,128)S(1)} collective-permute-done((f32[40,128]{1,0:T(8,128)}, f32[40,128]{1,0:T(8,128)S(1)}, u32[]{:S(2)}, u32[]{:S(2)}) %collective-permute-start) | collective-permute-done | bytes 20512 | tf_op jit(solution)/shard_map/ppermute | solution.py:349
  9.6 0.7 pad_maximum_fusion.2
  10.3 1.9 %collective-permute-start.1 = (f32[80,128]{1,0:T(8,128)S(1)}, f32[80,128]{1,0:T(8,128)S(1)}, u32[]{:S(2)}, u32[]{:S(2)}) collective-permute-start(f32[80,128]{1,0:T(8,128)S(1)} %pad_maximum_fusion.2), channel_id=1, source_target_pairs={{0,2},{1,3},{2,0},{3,1},{4,6},{5,7},{6,4},{7,5},{8,10},{9,11},{10,... | collective-permute-start | bytes 122888 | tf_op jit(solution)/shard_map/ppermute | solution.py:349
  12.2 0.7 constant_dynamic-update-slice_fusion.4
  12.9 1.4 %collective-permute-done.1 = f32[80,128]{1,0:T(8,128)S(1)} collective-permute-done((f32[80,128]{1,0:T(8,128)S(1)}, f32[80,128]{1,0:T(8,128)S(1)}, u32[]{:S(2)}, u32[]{:S(2)}) %collective-permute-start.1) | collective-permute-done | bytes 40992 | tf_op jit(solution)/shard_map/ppermute | solution.py:349
  14.3 0.7 pad_maximum_fusion.1
  15.0 1.9 %collective-permute-start.2 = (f32[160,128]{1,0:T(8,128)S(1)}, f32[160,128]{1,0:T(8,128)S(1)}, u32[]{:S(2)}, u32[]{:S(2)}) collective-permute-start(f32[160,128]{1,0:T(8,128)S(1)} %pad_maximum_fusion.1), channel_id=1, source_target_pairs={{0,1},{1,0},{2,3},{3,2},{4,5},{5,4},{6,7},{7,6},{8,9},{9,8},{10,11... | collective-permute-start | bytes 245768 | tf_op jit(solution)/shard_map/ppermute | solution.py:349
  17.0 2.5 %collective-permute-done.2 = f32[160,128]{1,0:T(8,128)S(1)} collective-permute-done((f32[160,128]{1,0:T(8,128)S(1)}, f32[160,128]{1,0:T(8,128)S(1)}, u32[]{:S(2)}, u32[]{:S(2)}) %collective-permute-start.2) | collective-permute-done | bytes 81952 | tf_op jit(solution)/shard_map/ppermute | solution.py:349
  19.5 0.7 pad_maximum_fusion
  20.2 2.0 %collective-permute-start.3 = (f32[320,128]{1,0:T(8,128)S(1)}, f32[320,128]{1,0:T(8,128)S(1)}, u32[]{:S(2)}, u32[]{:S(2)}) collective-permute-start(f32[320,128]{1,0:T(8,128)S(1)} %pad_maximum_fusion), channel_id=1, source_target_pairs={{0,16},{8,24},{16,0},{24,8},{1,17},{9,25},{17,1},{25,9},{2,18},{10... | collective-permute-start | bytes 491528 | tf_op jit(solution)/shard_map/ppermute | solution.py:349
  22.2 3.4 %collective-permute-done.3 = f32[320,128]{1,0:T(8,128)S(1)} collective-permute-done((f32[320,128]{1,0:T(8,128)S(1)}, f32[320,128]{1,0:T(8,128)S(1)}, u32[]{:S(2)}, u32[]{:S(2)}) %collective-permute-start.3) | collective-permute-done | bytes 163872 | tf_op jit(solution)/shard_map/ppermute | solution.py:349
  25.6 0.1 collective-permute-start.4
  25.7 0.7 reshape.12.resid_iface_ref
  26.4 0.9 collective-permute-done.4
  27.3 0.0 copy-start
  27.4 0.9 %copy-done = f32[1,256,256]{2,1,0:T(8,128)S(1)} copy-done((f32[1,256,256]{2,1,0:T(8,128)S(1)}, f32[1,256,256]{2,1,0:T(8,128)}, u32[]{:S(2)}) %copy-start) | copy-done | bytes 262168
  28.3 0.0 copy-start.1
  28.3 0.8 copy-done.1
  29.1 0.7 copy-done.2
  29.8 0.7 copy-done.3
  30.5 60.0 %shard_map.87 = (f32[1,256]{1,0:T(1,128)}, f32[1,1536]{1,0:T(1,128)S(1)}) custom-call(s32[1]{0:T(128)} %bitcast.me_ref, s32[1,64]{1,0:T(1,128)S(1)} %copy-done.3, s32[1]{0:T(128)S(6)} %copy.18.count_ref, f32[1280,128]{1,0:T(8,128)S(1)} %constant_dynamic-update-slice_fusion.5.pieces_ref, f32[1536,1536]{1,0:T(8,128)} %operator_ref.1, ...), custom_call_target="tpu_custom_call" | custom-call | tf_op jit(solution)/shard_map/pallas_call | solution.py:354
  90.5 0.6 constant_dynamic-slice_fusion
  (7 shorter events, 0.1 us)
Async XLA Ops:
  3.5 6.0 %collective-permute-start = (f32[40,128]{1,0:T(8,128)}, f32[40,128]{1,0:T(8,128)S(1)}, u32[]{:S(2)}, u32[]{:S(2)}) collective-permute-start(f32[40,128]{1,0:T(8,128)} %shard_map.86), channel_id=1, source_target_pairs={{0,4},{1,5},{2,6},{3,7},{4,0},{5,1},{6,2},{7,3},{8,12},{9,13},{10,... | collective-permute-start | bytes 61448 | tf_op jit(solution)/shard_map/ppermute | solution.py:349
  10.3 4.0 %collective-permute-start.1 = (f32[80,128]{1,0:T(8,128)S(1)}, f32[80,128]{1,0:T(8,128)S(1)}, u32[]{:S(2)}, u32[]{:S(2)}) collective-permute-start(f32[80,128]{1,0:T(8,128)S(1)} %pad_maximum_fusion.2), channel_id=1, source_target_pairs={{0,2},{1,3},{2,0},{3,1},{4,6},{5,7},{6,4},{7,5},{8,10},{9,11},{10,... | collective-permute-start | bytes 122888 | tf_op jit(solution)/shard_map/ppermute | solution.py:349
  15.0 4.4 %collective-permute-start.2 = (f32[160,128]{1,0:T(8,128)S(1)}, f32[160,128]{1,0:T(8,128)S(1)}, u32[]{:S(2)}, u32[]{:S(2)}) collective-permute-start(f32[160,128]{1,0:T(8,128)S(1)} %pad_maximum_fusion.1), channel_id=1, source_target_pairs={{0,1},{1,0},{2,3},{3,2},{4,5},{5,4},{6,7},{7,6},{8,9},{9,8},{10,11... | collective-permute-start | bytes 245768 | tf_op jit(solution)/shard_map/ppermute | solution.py:349
  20.2 5.4 %collective-permute-start.3 = (f32[320,128]{1,0:T(8,128)S(1)}, f32[320,128]{1,0:T(8,128)S(1)}, u32[]{:S(2)}, u32[]{:S(2)}) collective-permute-start(f32[320,128]{1,0:T(8,128)S(1)} %pad_maximum_fusion), channel_id=1, source_target_pairs={{0,16},{8,24},{16,0},{24,8},{1,17},{9,25},{17,1},{25,9},{2,18},{10... | collective-permute-start | bytes 491528 | tf_op jit(solution)/shard_map/ppermute | solution.py:349
  25.6 1.7 %collective-permute-start.4 = (f32[640,128]{1,0:T(8,128)S(1)}, f32[640,128]{1,0:T(8,128)S(1)}, u32[]{:S(2)}, u32[]{:S(2)}) collective-permute-start(f32[640,128]{1,0:T(8,128)S(1)} %get-tuple-element.6), channel_id=1, source_target_pairs={{0,8},{8,0},{16,24},{24,16},{1,9},{9,1},{17,25},{25,17},{2,10},{10... | collective-permute-start | bytes 983048 | tf_op jit(solution)/shard_map/ppermute | solution.py:349
  27.3 1.0 %copy-start = (f32[1,256,256]{2,1,0:T(8,128)S(1)}, f32[1,256,256]{2,1,0:T(8,128)}, u32[]{:S(2)}) copy-start(f32[1,256,256]{2,1,0:T(8,128)} %param.7) | copy-start | bytes 786436
  28.3 0.8 copy-start.1
  29.1 0.7 copy-start.2
  29.8 0.7 copy-start.3

commit v3 on v2

--- a/solution.py
+++ b/solution.py
@@ -10,12 +10,13 @@
 BF16 = jnp.bfloat16
 HIGHEST = lax.Precision.HIGHEST
 NB = 128
+BATCH = 4
 TB = 256
 NT = (((1,), (1,)), ((), ()))
 
 
 def lane_of(x, j):
-    return jnp.broadcast_to(x[:, j : j + 1], (8, 128))
+    return jnp.take_along_axis(x, jnp.full((8, 128), j, jnp.int32), axis=1, mode="promise_in_bounds")
 
 
 def row_of(x, i):
@@ -48,6 +49,7 @@
     sub = lax.broadcasted_iota(jnp.int32, (8, 128), 0)
     zero = jnp.zeros((8, 128), F32)
     is_row = [sub == p for p in range(8)]
+    scaled_rows = []
     own = [lane_of(T[0], j) for j in range(8)]
     after = [lane_of(T[1], j) for j in range(8)]
     ahead = [lane_of(T[1], 8 + j) for j in range(8)]
@@ -55,16 +57,23 @@
         last = g == groups - 1
         inside = (lane >= 8 * g) & (lane < 8 * g + 8)
         t = jnp.where(inside, jnp.where(lane - 8 * g == sub, 1.0, 0.0), T[g])
-        w = zero
-        inverses = zero
+        w, pivots, inverses = zero, zero, zero
         if not last:
             following = jnp.where(inside, zero, T[g + 1])
+        pivot = row_of(own[0], 0)
         for p in range(8):
-            pivot = row_of(own[p], p)
             r = 1.0 / pivot
-            f = jnp.where(is_row[p], 0.0, own[p] * r)
+            others = jnp.where(is_row[p], 0.0, own[p])
+            f = others * r
             across = [row_of(own[k], p) if k > p else None for k in range(8)]
             u = row_of(t, p)
+            w = jnp.where(is_row[p], u, w)
+            pivots = pivot if p == 0 else jnp.where(is_row[p], pivot, pivots)
+            if p < 7:
+                own[p + 1] = own[p + 1] - (others * across[p + 1]) * r
+                pivot = row_of(own[p + 1], p + 1)
+            for k in range(p + 2, 8):
+                own[k] = own[k] - f * across[k]
             if not last:
                 scaled = after[p] * r
                 for j in range(8):
@@ -72,11 +81,10 @@
                 for k in range(p + 1, 8):
                     after[k] = after[k] - scaled * across[k]
                 following = following - scaled * u
-            for k in range(p + 1, 8):
-                own[k] = own[k] - f * across[k]
-            w = jnp.where(is_row[p], u * lax.rsqrt(pivot), w)
             t = t - f * u
             inverses = jnp.where(is_row[p], r, inverses)
+        w = w * lax.rsqrt(pivots)
+        scaled_rows.append(w)
         W.append(jnp.where(lane < 8 * g + 8, w, 0.0))
         if not last:
             T[g + 1] = following
@@ -84,18 +92,35 @@
         if g + 2 < groups:
             E = t * inverses
             e = [row_of(E, p) for p in range(8)]
-            for i in range(g + 2, groups):
+            near = min(groups, BATCH * (g // BATCH + 2))
+            for i in range(g + 2, near):
                 old = T[i]
-                terms = [lane_of(old, 8 * g + j) * e[j] for j in range(8)]
-                while len(terms) > 1:
-                    terms = [x + y for x, y in zip(terms[::2], terms[1::2])]
-                T[i] = jnp.where(inside, zero, old) - terms[0]
+                T[i] = jnp.where(inside, zero, old)
+                for j in range(8):
+                    T[i] = T[i] - lane_of(old, 8 * g + j) * e[j]
             after = [lane_of(T[g + 2], 8 * (g + 1) + j) for j in range(8)]
             ahead = [lane_of(T[g + 2], 8 * (g + 2) + j) for j in range(8)]
+            if g % BATCH == BATCH - 1 and near < groups:
+                start = g - BATCH + 1
+                rows = [
+                    jnp.where((lane < 8 * q + 8) | (lane >= 8 * g + 8), scaled_rows[q], 0.0)
+                    for q in range(start, g + 1)
+                ]
+                rows = jnp.concatenate(rows, axis=0)
+                high, low = split(rows)
+                left_high, left_low = split(rows.T[8 * near : 8 * groups])
+
+                def plain(x, y):
+                    return lax.dot_general(x, y, (((1,), (0,)), ((), ())), preferred_element_type=F32)
+
+                far = plain(left_high, high) + (plain(left_high, low) + plain(left_low, high))
+                done = (lane >= 8 * start) & (lane < 8 * g + 8)
+                for i in range(near, groups):
+                    T[i] = jnp.where(done, zero, T[i]) - far[8 * (i - near) : 8 * (i - near) + 8]
         yield
 
 
-def piece_kernel(count_ref, coupling_ref, factor_ref, resid_ref, rows_ref, out_ref):
+def piece_kernel(count_ref, coupling_ref, factor_ref, resid_ref, piece_ref, rhs_ref):
     capacity, interior = coupling_ref.shape
     active = lax.broadcasted_iota(jnp.int32, (capacity, interior), 0) < count_ref[0]
     coupled = jnp.where(active, coupling_ref[...], 0.0)
@@ -104,31 +129,29 @@
     reduced = lax.dot_general(both, factor_ref[...], NT, precision=HIGHEST, preferred_element_type=F32)
     square = lax.dot_general(reduced, reduced[:capacity], NT, precision=HIGHEST, preferred_element_type=F32)
     half = capacity // 2
-    out_ref[0:half, 0:capacity] = square[0:half]
-    out_ref[0:half, capacity : 2 * capacity] = square[half:capacity]
-    out_ref[half : half + 8, 0:capacity] = square[capacity : capacity + 8]
-    out_ref[half : half + 8, capacity : 2 * capacity] = jnp.broadcast_to(
-        rows_ref[...].astype(F32), (8, capacity)
-    )
+    piece_ref[:, 0:capacity] = square[0:half]
+    piece_ref[:, capacity : 2 * capacity] = square[half:capacity]
+    rhs_ref[...] = square[capacity : capacity + 8]
 
 
 def system_kernel(
     steps,
     n,
+    blk,
     me_ref,
-    own_rows_ref,
     count_ref,
     pieces_ref,
-    operator_ref,
-    resid_iface_ref,
-    coupling_ref,
-    factor_ref,
-    resid_ref,
+    operator_hbm,
+    resid_iface_hbm,
+    coupling_hbm,
+    factor_hbm,
+    resid_hbm,
     interior_ref,
     iface_ref,
     M,
     by_row,
-    z_rows,
+    z_even,
+    z_odd,
     listed,
     listed_int,
     inverse,
@@ -138,9 +161,12 @@
     roots,
     x_columns,
     picked,
+    coupling_ref,
+    factor_ref,
+    resid_ref,
+    resid_iface_ref,
     listed_smem,
-    sem_operator,
-    sem_listed,
+    sems,
 ):
     S = M.shape[0]
     chunks = S // 128
@@ -151,8 +177,21 @@
     lane = lax.broadcasted_iota(jnp.int32, (8, 128), 1)
     sub = lax.broadcasted_iota(jnp.int32, (8, 128), 0)
 
-    get_operator = pltpu.make_async_copy(operator_ref, M, sem_operator)
+    get_operator = pltpu.make_async_copy(operator_hbm, M, sems.at[0])
     get_operator.start()
+    get_iface = [
+        pltpu.make_async_copy(
+            resid_iface_hbm.at[pl.ds(128 * c, 128)], resid_iface_ref.at[c], sems.at[5 + c]
+        )
+        for c in range(chunks)
+    ]
+    get_block = [
+        pltpu.make_async_copy(coupling_hbm, coupling_ref, sems.at[1]),
+        pltpu.make_async_copy(factor_hbm, factor_ref, sems.at[2]),
+        pltpu.make_async_copy(resid_hbm, resid_ref, sems.at[3]),
+    ]
+    for copy in get_iface + get_block:
+        copy.start()
 
     def slot_of(k):
         bits = k ^ me
@@ -167,7 +206,7 @@
 
     lax.fori_loop(0, n, list_rows, 0)
     listed_int[...] = listed[...].astype(jnp.int32)
-    get_listed = pltpu.make_async_copy(listed_int, listed_smem, sem_listed)
+    get_listed = pltpu.make_async_copy(listed_int, listed_smem, sems.at[4])
     get_listed.start()
 
     def clear(i, carry):
@@ -178,7 +217,7 @@
 
     def invert(b, carry):
         rows8 = listed_int[pl.ds(pl.multiple_of(b * 8, 8), 8), :]
-        found = [jnp.full((8, 128), -1, jnp.int32) for _ in range(chunks)]
+        found = [jnp.full((8, 128), capacity, jnp.int32) for _ in range(chunks)]
         for i in range(capacity):
             target = lane_of(rows8, capacity + i)
             for c in range(chunks):
@@ -190,45 +229,62 @@
     lax.fori_loop(0, n // 8, invert, 0)
     get_listed.wait()
 
-    rhs[...] = jnp.broadcast_to(resid_iface_ref[...], rhs.shape)
-
-    def scatter(k, carry):
+    for c, copy in enumerate(get_iface):
+        copy.wait()
+        rhs[:, 128 * c : 128 * (c + 1)] = jnp.broadcast_to(resid_iface_ref[c : c + 1, :], (16, 128))
+
+    def expand(k, z_rows):
         base = slot_of(k) * size
         strips = [pieces_ref[pl.ds(pl.multiple_of(base + 8 * s, 8), 8), :] for s in range(size // 8)]
+        strips = strips[:-1] + [pltpu.roll(x, capacity, 1) for x in strips[:-1]] + strips[-1:]
+        lower = lane < capacity
+        strips = [jnp.where(lower, x, 0.0) for x in strips]
         for c in range(chunks):
             at = jnp.broadcast_to(inverse[pl.ds(c * n + k, 1), :], (8, 128))
-            member = at >= 0
-            low = jnp.maximum(at, 0)
-            high = low + capacity
-            for s in range(half // 8):
-                for which, index in ((0, low), (half, high)):
-                    spread = jnp.take_along_axis(strips[s], index, axis=1, mode="promise_in_bounds")
-                    z_rows[pl.ds((which + 8 * s) * 16 + c, 8, stride=16), :] = jnp.where(member, spread, 0.0)
-            spread = jnp.take_along_axis(strips[half // 8], low, axis=1, mode="promise_in_bounds")
-            spread = jnp.where(member, spread, 0.0)
-            cols = slice(128 * c, 128 * (c + 1))
-            rhs[0:8, cols] = rhs[0:8, cols] + spread
+            for s, strip in enumerate(strips):
+                spread = jnp.take_along_axis(strip, at, axis=1, mode="promise_in_bounds")
+                if s < capacity // 8:
+                    z_rows[pl.ds(8 * s * chunks + c, 8, stride=chunks), :] = spread
+                else:
+                    cols = slice(128 * c, 128 * (c + 1))
+                    rhs[0:8, cols] = rhs[0:8, cols] + spread
+
+    def add_rows(k, z_rows):
         for i in range(0, capacity, 8):
-            places = [pl.multiple_of(listed_smem[k, capacity + i + u] * 16, 16) for u in range(8)]
+            places = [listed_smem[k, capacity + i + u] * chunks for u in range(8)]
             sums = [
-                by_row[pl.ds(places[u], 16), :] + z_rows[16 * (i + u) : 16 * (i + u + 1), :] for u in range(8)
+                by_row[pl.ds(places[u], chunks), :] + z_rows[chunks * (i + u) : chunks * (i + u + 1), :]
+                for u in range(8)
             ]
             for u in range(8):
-                by_row[pl.ds(places[u], 16), :] = sums[u]
+                by_row[pl.ds(places[u], chunks), :] = sums[u]
+
+    def scatter(pair, carry):
+        k = 2 * pair
+        expand(k + 1, z_odd)
+        add_rows(k, z_even)
+        expand(k + 2, z_even)
+        add_rows(k + 1, z_odd)
         return carry
 
-    lax.fori_loop(0, n, scatter, 0)
+    expand(0, z_even)
+    lax.fori_loop(0, n // 2 - 1, scatter, 0)
+    expand(n - 1, z_odd)
+    add_rows(n - 2, z_even)
+    add_rows(n - 1, z_odd)
     rhs[8:16, :] = rhs[0:8, :]
     get_operator.wait()
 
-    def assemble(q, carry):
-        row = pl.multiple_of(q * 8, 8)
-        for c in range(chunks):
-            cols = slice(128 * c, 128 * (c + 1))
-            M[pl.ds(row, 8), cols] = M[pl.ds(row, 8), cols] + by_row[pl.ds(row * 16 + c, 8, stride=16), :]
-        return carry
-
-    lax.fori_loop(0, S // 8, assemble, 0)
+    for part in range(chunks):
+
+        def assemble(q, carry, part=part):
+            row = pl.multiple_of(128 * part + q * 8, 8)
+            for c in range(part + 1):
+                cols = slice(128 * c, 128 * (c + 1))
+                M[pl.ds(row, 8), cols] = M[pl.ds(row, 8), cols] + by_row[pl.ds(row * chunks + c, 8, stride=chunks), :]
+            return carry
+
+        lax.fori_loop(0, 16, assemble, 0, unroll=2)
 
     panels = S // NB
 
@@ -293,14 +349,11 @@
         at = pl.multiple_of(j * NB, NB)
         t = jnp.broadcast_to(rhs[0:1, pl.ds(at, NB)], (8, NB))
         x = []
-        flat = jnp.zeros((8, 128), F32)
         for s in range(NB // 8):
             total = jnp.sum(roots[pl.ds(at + 8 * s, 8), :] * t, axis=1, keepdims=True)
             total = jnp.broadcast_to(total, (8, 128))
             x.append(total)
             x_columns[pl.ds(at + 8 * s, 8), :] = total
-            flat = flat + jnp.where(lane == sub + 8 * s, total, 0.0)
-        iface_ref[:, pl.ds(at, NB)] = jnp.sum(flat, axis=0, keepdims=True)
         for c in range(chunks):
             cols = slice(128 * c, 128 * (c + 1))
             total = x[0] * M[pl.ds(at, 8), cols]
@@ -311,8 +364,20 @@
 
     lax.fori_loop(0, panels, back, 0)
 
+    own = iface_ref.shape[1]
+    begin = (me & (blk - 1)) * own
+    for c in range(0, own, 128):
+        width = min(128, own - c)
+        flat = jnp.zeros((8, 128), F32)
+        for s in range(0, width, 8):
+            strip = x_columns[pl.ds(pl.multiple_of(begin + c + s, 8), 8), :]
+            flat = flat + jnp.where(lane == sub + s, strip, 0.0)
+        iface_ref[:, c : c + width] = jnp.sum(flat, axis=0, keepdims=True)[:, :width]
+
+    for copy in get_block:
+        copy.wait()
     for i in range(capacity):
-        picked[i : i + 1, :] = x_columns[pl.ds(own_rows_ref[0, i], 1), :]
+        picked[i : i + 1, :] = x_columns[pl.ds(listed_smem[me, capacity + i], 1), :]
     interior = coupling_ref.shape[1]
     corrected = []
     for c in range(interior // 128):
@@ -336,12 +401,17 @@
     anywhere = pl.BlockSpec(memory_space=pl.ANY)
     size = capacity // 2 + 8
 
-    gathered = pl.pallas_call(
+    piece, piece_rhs = pl.pallas_call(
         piece_kernel,
-        out_shape=jax.ShapeDtypeStruct((size, 2 * capacity), F32),
-        in_specs=[smem, vmem, vmem, vmem, vmem],
-        out_specs=vmem,
-    )(counts, couple, factor, resid_interior, iface_rows)
+        out_shape=(
+            jax.ShapeDtypeStruct((capacity // 2, 2 * capacity), F32),
+            jax.ShapeDtypeStruct((8, capacity), F32),
+        ),
+        in_specs=[smem, vmem, vmem, vmem],
+        out_specs=(vmem, vmem),
+    )(counts, couple, factor, resid_interior)
+    listed = jnp.broadcast_to(iface_rows.astype(F32), (8, capacity))
+    gathered = jnp.concatenate([piece, jnp.concatenate([piece_rhs, listed], axis=1)], axis=0)
 
     steps = []
     for axis, width, low in (("blk", blk, 0), ("leaf", leaf, blk.bit_length() - 1)):
@@ -352,17 +422,18 @@
 
     me = (lax.axis_index("leaf") * blk + lax.axis_index("blk")).astype(jnp.int32).reshape(1)
     interior_out, iface = pl.pallas_call(
-        functools.partial(system_kernel, tuple(steps), n),
+        functools.partial(system_kernel, tuple(steps), n, blk),
         out_shape=(
             jax.ShapeDtypeStruct((1, interior), F32),
-            jax.ShapeDtypeStruct((1, S), F32),
+            jax.ShapeDtypeStruct((1, S // blk), F32),
         ),
-        in_specs=[smem, smem, smem, vmem, anywhere, vmem, vmem, vmem, vmem],
+        in_specs=[smem, smem, vmem] + [anywhere] * 5,
         out_specs=(vmem, vmem),
         scratch_shapes=[
             pltpu.VMEM((S, S), F32),
-            pltpu.VMEM((S * 16, 128), F32),
-            pltpu.VMEM((capacity * 16, 128), F32),
+            pltpu.VMEM((S * S // 128, 128), F32),
+            pltpu.VMEM((capacity * S // 128, 128), F32),
+            pltpu.VMEM((capacity * S // 128, 128), F32),
             pltpu.VMEM((n, 128), F32),
             pltpu.VMEM((n, 128), jnp.int32),
             pltpu.VMEM((n * S // 128, 128), jnp.int32),
@@ -372,25 +443,25 @@
             pltpu.VMEM((S, NB), F32),
             pltpu.VMEM((S, 128), F32),
             pltpu.VMEM((capacity, 128), F32),
+            pltpu.VMEM((capacity, interior), F32),
+            pltpu.VMEM((interior, interior), F32),
+            pltpu.VMEM((1, interior), F32),
+            pltpu.VMEM((S // 128, 128), F32),
             pltpu.SMEM((n, 128), jnp.int32),
-            pltpu.SemaphoreType.DMA,
-            pltpu.SemaphoreType.DMA,
+            pltpu.SemaphoreType.DMA((5 + S // 128,)),
         ],
         compiler_params=pltpu.CompilerParams(vmem_limit_bytes=48 * 1024 * 1024),
     )(
         me,
-        iface_rows,
         counts,
         gathered,
         iface_operator,
-        resid_iface.reshape(1, S),
+        resid_iface,
         couple,
         factor,
         resid_interior,
     )
-    own = S // blk
-    own_part = lax.dynamic_slice_in_dim(iface[0], lax.axis_index("blk") * own, own, 0)
-    return interior_out, own_part
+    return interior_out, iface.reshape(S // blk)
 
 
 def solution(mesh):

time: 91.6 us -> 79.8 us (0.87)
  Pallas kernels: 62.2 us -> 49.9 us
  other arithmetic: 2.21 us -> 3.8 us
  local copies, waits for them, and re-layouts: 5.26 us -> 3.96 us
    pallas_call x2, Pallas kernels: 62.2 us -> 49.9 us  [the longest x1 47.6 us: shards(): pl.pallas_call(functools.partial(system_kernel, tuple(steps), n, blk), ou...]
    concatenate x3 -> x2, other arithmetic: 2.21 us -> 1.59 us  [shards(): gathered = jnp.concatenate([gathered, other], axis=0)]
where the time goes in v3:
time: 79.8 us; the launch traced here: 79 us
  Pallas kernels  49.9 us (63%)
  starting transfers between devices  9.92 us (12%)
  waiting for transfers between devices  9.9 us (12%)
  local copies, waits for them, and re-layouts  3.96 us (5%)
  other arithmetic  3.8 us (5%)
  between operations  1.53 us (2%)
    pallas_call x1, Pallas kernels, shards(): pl.pallas_call(functools.partial(system_kernel, tuple(steps), n, blk), ou...  47.6 us
    ppermute x5, starting transfers between devices, shards(): lax.ppermute(gathered, axis, [(i, i ^ 1 << bit) for i in range(width)])  9.92 us
    ppermute x5, waiting for transfers between devices, shards(): lax.ppermute(gathered, axis, [(i, i ^ 1 << bit) for i in range(width)])  9.9 us
    unnamed x12, local copies, waits for them, and re-layouts  3.91 us
    pallas_call x1, Pallas kernels, shards(): pl.pallas_call(piece_kernel, out_shape=(jax.ShapeDtypeStruct((capacity //...  2.25 us
  transfers between devices with their start and end apart: 5, of which 5 were waited for; matrix products, arithmetic and copies ran while one was open for 2% of the time, Pallas kernels for 0%

profile of v3, /device:TPU:0, one launch (start us, length us, event | category | flops | bytes accessed | tf_op | source)
XLA Modules:
  0.0 79.0 jit_solution(8558863060077209189)
XLA Ops:
  1.3 0.7 convert_bitcast_fusion
  1.9 2.2 %shard_map.86 = (f32[32,128]{1,0:T(8,128)}, f32[8,64]{1,0:T(8,128)}) custom-call(s32[1]{0:T(128)S(6)} %copy.24.count_ref, f32[64,256]{1,0:T(8,128)} %bitcast.8, f32[256,256]{1,0:T(8,128)} %bitcast.6, f32[1,256]{1,0:T(1,128)} %resid_hbm.1), custom_call_target="tpu_custom_call" | custom-call | tf_op jit(solution)/shard_map/pallas_call | solution.py:404
  4.2 0.8 %maximum_maximum_fusion = f32[40,128]{1,0:T(8,128)S(1)} fusion(f32[8,64]{1,0:T(8,128)S(1)} %broadcast_in_dim.8, f32[8,64]{1,0:T(8,128)} %get-tuple-element.7, f32[32,128]{1,0:T(8,128)} %get-tuple-element.6), kind=kLoop, calls=%fused_computation.20 | loop fusion | flops 10240 | bytes 40960 | tf_op jit(solution)/shard_map/concatenate | solution.py:414
  5.0 4.0 %collective-permute-start = (f32[40,128]{1,0:T(8,128)S(1)}, f32[40,128]{1,0:T(8,128)S(1)}, u32[]{:S(2)}, u32[]{:S(2)}) collective-permute-start(f32[40,128]{1,0:T(8,128)S(1)} %maximum_maximum_fusion), channel_id=1, source_target_pairs={{0,4},{1,5},{2,6},{3,7},{4,0},{5,1},{6,2},{7,3},{8,12},{9,13},{10,... | collective-permute-start | bytes 61448 | tf_op jit(solution)/shard_map/ppermute | solution.py:419
  9.0 0.7 constant_dynamic-update-slice_fusion.10
  9.7 0.8 constant_dynamic-update-slice_fusion.9
  10.5 0.3 collective-permute-done
  10.8 0.8 %pad_maximum_fusion.1 = f32[80,128]{1,0:T(8,128)S(1)} fusion(f32[40,128]{1,0:T(8,128)S(1)} %collective-permute-done, f32[8,64]{1,0:T(8,128)S(1)} %broadcast_in_dim.8, f32[8,64]{1,0:T(8,128)} %get-tuple-element.7, f32[32,128]{1,0:T(8,128)} %get-tuple-element.6), kind=kLoop, calls=%fused_computation.1 | loop fusion | flops 30720 | bytes 81920 | tf_op jit(solution)/shard_map/concatenate | solution.py:420
  11.6 1.9 %collective-permute-start.1 = (f32[80,128]{1,0:T(8,128)S(1)}, f32[80,128]{1,0:T(8,128)S(1)}, u32[]{:S(2)}, u32[]{:S(2)}) collective-permute-start(f32[80,128]{1,0:T(8,128)S(1)} %pad_maximum_fusion.1), channel_id=1, source_target_pairs={{0,2},{1,3},{2,0},{3,1},{4,6},{5,7},{6,4},{7,5},{8,10},{9,11},{10,... | collective-permute-start | bytes 122888 | tf_op jit(solution)/shard_map/ppermute | solution.py:419
  13.5 2.1 %collective-permute-done.1 = f32[80,128]{1,0:T(8,128)S(1)} collective-permute-done((f32[80,128]{1,0:T(8,128)S(1)}, f32[80,128]{1,0:T(8,128)S(1)}, u32[]{:S(2)}, u32[]{:S(2)}) %collective-permute-start.1) | collective-permute-done | bytes 40992 | tf_op jit(solution)/shard_map/ppermute | solution.py:419
  15.6 0.8 %pad_maximum_fusion = f32[160,128]{1,0:T(8,128)S(1)} fusion(f32[80,128]{1,0:T(8,128)S(1)} %collective-permute-done.1, f32[40,128]{1,0:T(8,128)S(1)} %collective-permute-done, f32[8,64]{1,0:T(8,128)S(1)} %broadcast_in_dim.8, f32[8,64]{1,0:T(8,128)} %get-tuple-element.7, f32[32,128]{1,0:T(8,128)} %get-tuple-element.6), kind=kLoop, calls=%fused_computation | loop fusion | flops 81920 | bytes 163840 | tf_op jit(solution)/shard_map/concatenate | solution.py:420
  16.4 1.9 %collective-permute-start.2 = (f32[160,128]{1,0:T(8,128)S(1)}, f32[160,128]{1,0:T(8,128)S(1)}, u32[]{:S(2)}, u32[]{:S(2)}) collective-permute-start(f32[160,128]{1,0:T(8,128)S(1)} %pad_maximum_fusion), channel_id=1, source_target_pairs={{0,1},{1,0},{2,3},{3,2},{4,5},{5,4},{6,7},{7,6},{8,9},{9,8},{10,11... | collective-permute-start | bytes 245768 | tf_op jit(solution)/shard_map/ppermute | solution.py:419
  18.3 2.5 %collective-permute-done.2 = f32[160,128]{1,0:T(8,128)S(1)} collective-permute-done((f32[160,128]{1,0:T(8,128)S(1)}, f32[160,128]{1,0:T(8,128)S(1)}, u32[]{:S(2)}, u32[]{:S(2)}) %collective-permute-start.2) | collective-permute-done | bytes 81952 | tf_op jit(solution)/shard_map/ppermute | solution.py:419
  20.8 2.0 %collective-permute-start.3 = (f32[320,128]{1,0:T(8,128)S(1)}, f32[320,128]{1,0:T(8,128)S(1)}, u32[]{:S(2)}, u32[]{:S(2)}) collective-permute-start(f32[320,128]{1,0:T(8,128)S(1)} %get-tuple-element.14), channel_id=1, source_target_pairs={{0,16},{8,24},{16,0},{24,8},{1,17},{9,25},{17,1},{25,9},{2,18},{10... | collective-permute-start | bytes 491528 | tf_op jit(solution)/shard_map/ppermute | solution.py:419
  22.8 3.4 %collective-permute-done.3 = f32[320,128]{1,0:T(8,128)S(1)} collective-permute-done((f32[320,128]{1,0:T(8,128)S(1)}, f32[320,128]{1,0:T(8,128)S(1)}, u32[]{:S(2)}, u32[]{:S(2)}) %collective-permute-start.3) | collective-permute-done | bytes 163872 | tf_op jit(solution)/shard_map/ppermute | solution.py:419
  26.3 0.1 collective-permute-start.4
  26.3 1.6 %collective-permute-done.4 = f32[640,128]{1,0:T(8,128)S(1)} collective-permute-done((f32[640,128]{1,0:T(8,128)S(1)}, f32[640,128]{1,0:T(8,128)S(1)}, u32[]{:S(2)}, u32[]{:S(2)}) %collective-permute-start.4) | collective-permute-done | bytes 327712 | tf_op jit(solution)/shard_map/ppermute | solution.py:419
  28.0 0.0 copy-start
  28.0 0.9 %copy-done = f32[1,256,256]{2,1,0:T(8,128)S(1)} copy-done((f32[1,256,256]{2,1,0:T(8,128)S(1)}, f32[1,256,256]{2,1,0:T(8,128)}, u32[]{:S(2)}) %copy-start) | copy-done | bytes 262168
  28.9 0.0 copy-start.1
  28.9 0.8 %copy-done.1 = f32[1,64,256]{2,1,0:T(8,128)S(1)} copy-done((f32[1,64,256]{2,1,0:T(8,128)S(1)}, f32[1,64,256]{2,1,0:T(8,128)}, u32[]{:S(2)}) %copy-start.1) | copy-done | bytes 65560
  29.8 0.7 copy-done.2
  30.5 0.7 copy-done.3
  31.2 47.6 %shard_map.87 = (f32[1,256]{1,0:T(1,128)}, f32[1,192]{1,0:T(1,128)}) custom-call(s32[1]{0:T(128)} %bitcast.me_ref, s32[1]{0:T(128)S(6)} %copy.24.count_ref, f32[1280,128]{1,0:T(8,128)S(1)} %constant_dynamic-update-slice_fusion.11.pieces_ref, f32[1536,1536]{1,0:T(8,128)} %operator_hbm.1, f32[1536]{0:T(1024)S(1)} %copy-done.2, f32[64,256]{1,0:T(8,128)S(1)} %bitcast.9, ...), custom_call_target="tpu_custom_call" | custom-call | tf_op jit(solution)/shard_map/pallas_call | solution.py:424
  (8 shorter events, 0.1 us)
Async XLA Ops:
  5.0 5.8 %collective-permute-start = (f32[40,128]{1,0:T(8,128)S(1)}, f32[40,128]{1,0:T(8,128)S(1)}, u32[]{:S(2)}, u32[]{:S(2)}) collective-permute-start(f32[40,128]{1,0:T(8,128)S(1)} %maximum_maximum_fusion), channel_id=1, source_target_pairs={{0,4},{1,5},{2,6},{3,7},{4,0},{5,1},{6,2},{7,3},{8,12},{9,13},{10,... | collective-permute-start | bytes 61448 | tf_op jit(solution)/shard_map/ppermute | solution.py:419
  11.6 4.0 %collective-permute-start.1 = (f32[80,128]{1,0:T(8,128)S(1)}, f32[80,128]{1,0:T(8,128)S(1)}, u32[]{:S(2)}, u32[]{:S(2)}) collective-permute-start(f32[80,128]{1,0:T(8,128)S(1)} %pad_maximum_fusion.1), channel_id=1, source_target_pairs={{0,2},{1,3},{2,0},{3,1},{4,6},{5,7},{6,4},{7,5},{8,10},{9,11},{10,... | collective-permute-start | bytes 122888 | tf_op jit(solution)/shard_map/ppermute | solution.py:419
  16.4 4.4 %collective-permute-start.2 = (f32[160,128]{1,0:T(8,128)S(1)}, f32[160,128]{1,0:T(8,128)S(1)}, u32[]{:S(2)}, u32[]{:S(2)}) collective-permute-start(f32[160,128]{1,0:T(8,128)S(1)} %pad_maximum_fusion), channel_id=1, source_target_pairs={{0,1},{1,0},{2,3},{3,2},{4,5},{5,4},{6,7},{7,6},{8,9},{9,8},{10,11... | collective-permute-start | bytes 245768 | tf_op jit(solution)/shard_map/ppermute | solution.py:419
  20.8 5.4 %collective-permute-start.3 = (f32[320,128]{1,0:T(8,128)S(1)}, f32[320,128]{1,0:T(8,128)S(1)}, u32[]{:S(2)}, u32[]{:S(2)}) collective-permute-start(f32[320,128]{1,0:T(8,128)S(1)} %get-tuple-element.14), channel_id=1, source_target_pairs={{0,16},{8,24},{16,0},{24,8},{1,17},{9,25},{17,1},{25,9},{2,18},{10... | collective-permute-start | bytes 491528 | tf_op jit(solution)/shard_map/ppermute | solution.py:419
  26.3 1.7 %collective-permute-start.4 = (f32[640,128]{1,0:T(8,128)S(1)}, f32[640,128]{1,0:T(8,128)S(1)}, u32[]{:S(2)}, u32[]{:S(2)}) collective-permute-start(f32[640,128]{1,0:T(8,128)S(1)} %get-tuple-element.10), channel_id=1, source_target_pairs={{0,8},{8,0},{16,24},{24,16},{1,9},{9,1},{17,25},{25,17},{2,10},{10... | collective-permute-start | bytes 983048 | tf_op jit(solution)/shard_map/ppermute | solution.py:419
  28.0 1.0 %copy-start = (f32[1,256,256]{2,1,0:T(8,128)S(1)}, f32[1,256,256]{2,1,0:T(8,128)}, u32[]{:S(2)}) copy-start(f32[1,256,256]{2,1,0:T(8,128)} %param.7) | copy-start | bytes 786436
  28.9 0.8 %copy-start.1 = (f32[1,64,256]{2,1,0:T(8,128)S(1)}, f32[1,64,256]{2,1,0:T(8,128)}, u32[]{:S(2)}) copy-start(f32[1,64,256]{2,1,0:T(8,128)} %param.8) | copy-start | bytes 196612
  29.8 0.7 copy-start.2
  30.5 0.7 copy-start.3

commit v4 on v3

--- a/solution.py
+++ b/solution.py
@@ -120,18 +120,45 @@
         yield
 
 
-def piece_kernel(count_ref, coupling_ref, factor_ref, resid_ref, piece_ref, rhs_ref):
+def piece_kernel(
+    count_ref,
+    coupling_ref,
+    factor_ref,
+    resid_ref,
+    rows_ref,
+    resid_iface_hbm,
+    out_ref,
+    coupled_ref,
+    factor_out_ref,
+    resid_out_ref,
+    iface_out_ref,
+    sems,
+):
+    get_iface = [
+        pltpu.make_async_copy(resid_iface_hbm.at[pl.ds(128 * c, 128)], iface_out_ref.at[c], sems.at[c])
+        for c in range(iface_out_ref.shape[0])
+    ]
+    for copy in get_iface:
+        copy.start()
     capacity, interior = coupling_ref.shape
     active = lax.broadcasted_iota(jnp.int32, (capacity, interior), 0) < count_ref[0]
     coupled = jnp.where(active, coupling_ref[...], 0.0)
+    coupled_ref[...] = coupled
+    factor_out_ref[...] = factor_ref[...]
+    resid_out_ref[...] = resid_ref[...]
     extra = jnp.broadcast_to(resid_ref[...], (8, interior))
     both = jnp.concatenate([coupled, extra], axis=0)
     reduced = lax.dot_general(both, factor_ref[...], NT, precision=HIGHEST, preferred_element_type=F32)
     square = lax.dot_general(reduced, reduced[:capacity], NT, precision=HIGHEST, preferred_element_type=F32)
     half = capacity // 2
-    piece_ref[:, 0:capacity] = square[0:half]
-    piece_ref[:, capacity : 2 * capacity] = square[half:capacity]
-    rhs_ref[...] = square[capacity : capacity + 8]
+    out_ref[0:half, 0:capacity] = square[0:half]
+    out_ref[0:half, capacity : 2 * capacity] = square[half:capacity]
+    out_ref[half : half + 8, 0:capacity] = square[capacity : capacity + 8]
+    out_ref[half : half + 8, capacity : 2 * capacity] = jnp.broadcast_to(
+        rows_ref[...].astype(F32), (8, capacity)
+    )
+    for copy in get_iface:
+        copy.wait()
 
 
 def system_kernel(
@@ -139,13 +166,12 @@
     n,
     blk,
     me_ref,
-    count_ref,
     pieces_ref,
     operator_hbm,
-    resid_iface_hbm,
-    coupling_hbm,
-    factor_hbm,
-    resid_hbm,
+    coupled_ref,
+    factor_ref,
+    resid_ref,
+    resid_iface_ref,
     interior_ref,
     iface_ref,
     M,
@@ -161,16 +187,12 @@
     roots,
     x_columns,
     picked,
-    coupling_ref,
-    factor_ref,
-    resid_ref,
-    resid_iface_ref,
     listed_smem,
     sems,
 ):
     S = M.shape[0]
     chunks = S // 128
-    capacity = coupling_ref.shape[0]
+    capacity = coupled_ref.shape[0]
     half = capacity // 2
     size = half + 8
     me = me_ref[0]
@@ -179,20 +201,6 @@
 
     get_operator = pltpu.make_async_copy(operator_hbm, M, sems.at[0])
     get_operator.start()
-    get_iface = [
-        pltpu.make_async_copy(
-            resid_iface_hbm.at[pl.ds(128 * c, 128)], resid_iface_ref.at[c], sems.at[5 + c]
-        )
-        for c in range(chunks)
-    ]
-    get_block = [
-        pltpu.make_async_copy(coupling_hbm, coupling_ref, sems.at[1]),
-        pltpu.make_async_copy(factor_hbm, factor_ref, sems.at[2]),
-        pltpu.make_async_copy(resid_hbm, resid_ref, sems.at[3]),
-    ]
-    for copy in get_iface + get_block:
-        copy.start()
-
     def slot_of(k):
         bits = k ^ me
         slot = 0
@@ -206,7 +214,7 @@
 
     lax.fori_loop(0, n, list_rows, 0)
     listed_int[...] = listed[...].astype(jnp.int32)
-    get_listed = pltpu.make_async_copy(listed_int, listed_smem, sems.at[4])
+    get_listed = pltpu.make_async_copy(listed_int, listed_smem, sems.at[1])
     get_listed.start()
 
     def clear(i, carry):
@@ -229,8 +237,7 @@
     lax.fori_loop(0, n // 8, invert, 0)
     get_listed.wait()
 
-    for c, copy in enumerate(get_iface):
-        copy.wait()
+    for c in range(chunks):
         rhs[:, 128 * c : 128 * (c + 1)] = jnp.broadcast_to(resid_iface_ref[c : c + 1, :], (16, 128))
 
     def expand(k, z_rows):
@@ -344,25 +351,19 @@
     for item in work:
         item()
 
-    def back(step, carry):
-        j = panels - 1 - step
-        at = pl.multiple_of(j * NB, NB)
-        t = jnp.broadcast_to(rhs[0:1, pl.ds(at, NB)], (8, NB))
+    for j in reversed(range(panels)):
+        t = jnp.broadcast_to(rhs[0:1, block(j)], (8, NB))
         x = []
-        for s in range(NB // 8):
-            total = jnp.sum(roots[pl.ds(at + 8 * s, 8), :] * t, axis=1, keepdims=True)
-            total = jnp.broadcast_to(total, (8, 128))
-            x.append(total)
-            x_columns[pl.ds(at + 8 * s, 8), :] = total
-        for c in range(chunks):
-            cols = slice(128 * c, 128 * (c + 1))
-            total = x[0] * M[pl.ds(at, 8), cols]
-            for s in range(1, NB // 8):
-                total = total + x[s] * M[pl.ds(at + 8 * s, 8), cols]
-            rhs[0:1, cols] = rhs[0:1, cols] - jnp.sum(total, axis=0, keepdims=True)
-        return carry
-
-    lax.fori_loop(0, panels, back, 0)
+        for q in range(NB * j, NB * (j + 1), 8):
+            total = jnp.sum(roots[q : q + 8, :] * t, axis=1, keepdims=True)
+            x.append(jnp.broadcast_to(total, (8, 128)))
+            x_columns[q : q + 8, :] = x[-1]
+        for i in reversed(range(j)):
+            total = None
+            for at, q in enumerate(range(NB * j, NB * (j + 1), 8)):
+                term = x[at] * M[q : q + 8, block(i)]
+                total = term if total is None else total + term
+            rhs[0:1, block(i)] = rhs[0:1, block(i)] - jnp.sum(total, axis=0, keepdims=True)
 
     own = iface_ref.shape[1]
     begin = (me & (blk - 1)) * own
@@ -374,16 +375,13 @@
             flat = flat + jnp.where(lane == sub + s, strip, 0.0)
         iface_ref[:, c : c + width] = jnp.sum(flat, axis=0, keepdims=True)[:, :width]
 
-    for copy in get_block:
-        copy.wait()
     for i in range(capacity):
         picked[i : i + 1, :] = x_columns[pl.ds(listed_smem[me, capacity + i], 1), :]
-    interior = coupling_ref.shape[1]
+    interior = coupled_ref.shape[1]
     corrected = []
     for c in range(interior // 128):
         cols = slice(128 * c, 128 * (c + 1))
-        row = lax.broadcasted_iota(jnp.int32, (capacity, 128), 0)
-        terms = jnp.where(row < count_ref[0], coupling_ref[:, cols] * picked[...], 0.0)
+        terms = coupled_ref[:, cols] * picked[...]
         corrected.append(resid_ref[:, cols] - jnp.sum(terms, axis=0, keepdims=True))
     corrected = jnp.concatenate(corrected, axis=1)
     inner = jnp.sum(factor_ref[...] * corrected, axis=1, keepdims=True)
@@ -398,20 +396,22 @@
     n = leaf * blk
     vmem = pl.BlockSpec(memory_space=pltpu.VMEM)
     smem = pl.BlockSpec(memory_space=pltpu.SMEM)
-    anywhere = pl.BlockSpec(memory_space=pl.ANY)
+    anywhere = pl.BlockSpec(memory_space=pltpu.HBM)
     size = capacity // 2 + 8
 
-    piece, piece_rhs = pl.pallas_call(
+    gathered, coupled, factor, resid, iface_rhs = pl.pallas_call(
         piece_kernel,
         out_shape=(
-            jax.ShapeDtypeStruct((capacity // 2, 2 * capacity), F32),
-            jax.ShapeDtypeStruct((8, capacity), F32),
+            pltpu.VMEM((size, 2 * capacity), F32),
+            pltpu.VMEM((capacity, interior), F32),
+            pltpu.VMEM((interior, interior), F32),
+            pltpu.VMEM((1, interior), F32),
+            pltpu.VMEM((S // 128, 128), F32),
         ),
-        in_specs=[smem, vmem, vmem, vmem],
-        out_specs=(vmem, vmem),
-    )(counts, couple, factor, resid_interior)
-    listed = jnp.broadcast_to(iface_rows.astype(F32), (8, capacity))
-    gathered = jnp.concatenate([piece, jnp.concatenate([piece_rhs, listed], axis=1)], axis=0)
+        in_specs=[smem, vmem, vmem, vmem, vmem, anywhere],
+        out_specs=(vmem,) * 5,
+        scratch_shapes=[pltpu.SemaphoreType.DMA((S // 128,))],
+    )(counts, couple, factor, resid_interior, iface_rows, resid_iface)
 
     steps = []
     for axis, width, low in (("blk", blk, 0), ("leaf", leaf, blk.bit_length() - 1)):
@@ -427,7 +427,7 @@
             jax.ShapeDtypeStruct((1, interior), F32),
             jax.ShapeDtypeStruct((1, S // blk), F32),
         ),
-        in_specs=[smem, smem, vmem] + [anywhere] * 5,
+        in_specs=[smem, vmem, anywhere, vmem, vmem, vmem, vmem],
         out_specs=(vmem, vmem),
         scratch_shapes=[
             pltpu.VMEM((S, S), F32),
@@ -443,23 +443,18 @@
             pltpu.VMEM((S, NB), F32),
             pltpu.VMEM((S, 128), F32),
             pltpu.VMEM((capacity, 128), F32),
-            pltpu.VMEM((capacity, interior), F32),
-            pltpu.VMEM((interior, interior), F32),
-            pltpu.VMEM((1, interior), F32),
-            pltpu.VMEM((S // 128, 128), F32),
             pltpu.SMEM((n, 128), jnp.int32),
-            pltpu.SemaphoreType.DMA((5 + S // 128,)),
+            pltpu.SemaphoreType.DMA((2,)),
         ],
         compiler_params=pltpu.CompilerParams(vmem_limit_bytes=48 * 1024 * 1024),
     )(
         me,
-        counts,
         gathered,
         iface_operator,
-        resid_iface,
-        couple,
+        coupled,
         factor,
-        resid_interior,
+        resid,
+        iface_rhs,
     )
     return interior_out, iface.reshape(S // blk)
 

time: 79.8 us -> 72.1 us (0.904)
  local copies, waits for them, and re-layouts: 3.96 us -> 0.07 us
  other arithmetic: 3.8 us -> 0.02 us
  waiting for transfers between devices: 9.9 us -> 11.4 us
  Pallas kernels: 49.9 us -> 48.9 us
    unnamed x12 -> x4, local copies, waits for them, and re-layouts: 3.91 us -> 0.03 us
    concatenate x2 -> x3, other arithmetic: 1.59 us -> 0.02 us  [shards(): gathered = jnp.concatenate([gathered, other], axis=0)]
    ppermute x5, waiting for transfers between devices: 9.9 us -> 11.4 us  [shards(): lax.ppermute(gathered, axis, [(i, i ^ 1 << bit) for i in range(width)])]
  transfers between devices with their start and end apart: 5 -> 5, of which waited for: 5 -> 5; matrix products, arithmetic and copies ran while one was open for 2% -> 0% of each run, Pallas kernels for 0% -> 0%
where the time goes in v4:
time: 72.1 us; the launch traced here: 71.9 us
  Pallas kernels  48.9 us (68%)
  waiting for transfers between devices  11.4 us (16%)
  starting transfers between devices  9.98 us (14%)
  between operations  1.5 us (2%)
    pallas_call x1, Pallas kernels, shards(): pl.pallas_call(functools.partial(system_kernel, tuple(steps), n, blk), ou...  47 us
    ppermute x5, waiting for transfers between devices, shards(): lax.ppermute(gathered, axis, [(i, i ^ 1 << bit) for i in range(width)])  11.4 us
    ppermute x5, starting transfers between devices, shards(): lax.ppermute(gathered, axis, [(i, i ^ 1 << bit) for i in range(width)])  9.98 us
    pallas_call x1, Pallas kernels, shards(): pl.pallas_call(piece_kernel, out_shape=(pltpu.VMEM((size, 2 * capacity),...  1.89 us
  transfers between devices with their start and end apart: 5, of which 5 were waited for; matrix products, arithmetic and copies ran while one was open for 0% of the time, Pallas kernels for 0%

profile of v4, /device:TPU:0, one launch (start us, length us, event | category | flops | bytes accessed | tf_op | source)
XLA Modules:
  0.0 71.9 jit_solution(13137980580555084879)
XLA Ops:
  1.3 1.9 %shard_map.86 = (f32[40,128]{1,0:T(8,128)S(1)}, f32[64,256]{1,0:T(8,128)S(1)}, f32[256,256]{1,0:T(8,128)S(1)}, f32[1,256]{1,0:T(1,128)S(1)}, f32[12,128]{1,0:T(8,128)S(1)}) custom-call(s32[1]{0:T(128)S(6)} %copy.18.count_ref, f32[64,256]{1,0:T(8,128)} %bitcast.5, f32[256,256]{1,0:T(8,128)} %bitcast.4, f32[1,256]{1,0:T(1,128)} %resid_ref.1, ...), custom_call_target="tpu_custom_call" | custom-call | tf_op jit(solution)/shard_map/pallas_call | solution.py:402
  3.2 4.1 %collective-permute-start = (f32[40,128]{1,0:T(8,128)S(1)}, f32[40,128]{1,0:T(8,128)S(1)}, u32[]{:S(2)}, u32[]{:S(2)}) collective-permute-start(f32[40,128]{1,0:T(8,128)S(1)} %get-tuple-element.9), channel_id=1, source_target_pairs={{0,4},{1,5},{2,6},{3,7},{4,0},{5,1},{6,2},{7,3},{8,12},{9,13},{10,... | collective-permute-start | bytes 61448 | tf_op jit(solution)/shard_map/ppermute | solution.py:419
  7.3 1.8 %collective-permute-done = f32[40,128]{1,0:T(8,128)S(1)} collective-permute-done((f32[40,128]{1,0:T(8,128)S(1)}, f32[40,128]{1,0:T(8,128)S(1)}, u32[]{:S(2)}, u32[]{:S(2)}) %collective-permute-start) | collective-permute-done | bytes 20512 | tf_op jit(solution)/shard_map/ppermute | solution.py:419
  9.1 1.9 %collective-permute-start.1 = (f32[80,128]{1,0:T(8,128)S(1)}, f32[80,128]{1,0:T(8,128)S(1)}, u32[]{:S(2)}, u32[]{:S(2)}) collective-permute-start(f32[80,128]{1,0:T(8,128)S(1)} %pad_maximum_fusion.2), channel_id=1, source_target_pairs={{0,2},{1,3},{2,0},{3,1},{4,6},{5,7},{6,4},{7,5},{8,10},{9,11},{10,... | collective-permute-start | bytes 122888 | tf_op jit(solution)/shard_map/ppermute | solution.py:419
  11.0 2.1 %collective-permute-done.1 = f32[80,128]{1,0:T(8,128)S(1)} collective-permute-done((f32[80,128]{1,0:T(8,128)S(1)}, f32[80,128]{1,0:T(8,128)S(1)}, u32[]{:S(2)}, u32[]{:S(2)}) %collective-permute-start.1) | collective-permute-done | bytes 40992 | tf_op jit(solution)/shard_map/ppermute | solution.py:419
  13.1 1.9 %collective-permute-start.2 = (f32[160,128]{1,0:T(8,128)S(1)}, f32[160,128]{1,0:T(8,128)S(1)}, u32[]{:S(2)}, u32[]{:S(2)}) collective-permute-start(f32[160,128]{1,0:T(8,128)S(1)} %pad_maximum_fusion.1), channel_id=1, source_target_pairs={{0,1},{1,0},{2,3},{3,2},{4,5},{5,4},{6,7},{7,6},{8,9},{9,8},{10,11... | collective-permute-start | bytes 245768 | tf_op jit(solution)/shard_map/ppermute | solution.py:419
  15.0 2.5 %collective-permute-done.2 = f32[160,128]{1,0:T(8,128)S(1)} collective-permute-done((f32[160,128]{1,0:T(8,128)S(1)}, f32[160,128]{1,0:T(8,128)S(1)}, u32[]{:S(2)}, u32[]{:S(2)}) %collective-permute-start.2) | collective-permute-done | bytes 81952 | tf_op jit(solution)/shard_map/ppermute | solution.py:419
  17.5 2.0 %collective-permute-start.3 = (f32[320,128]{1,0:T(8,128)S(1)}, f32[320,128]{1,0:T(8,128)S(1)}, u32[]{:S(2)}, u32[]{:S(2)}) collective-permute-start(f32[320,128]{1,0:T(8,128)S(1)} %pad_maximum_fusion), channel_id=1, source_target_pairs={{0,16},{8,24},{16,0},{24,8},{1,17},{9,25},{17,1},{25,9},{2,18},{10... | collective-permute-start | bytes 491528 | tf_op jit(solution)/shard_map/ppermute | solution.py:419
  19.5 3.4 %collective-permute-done.3 = f32[320,128]{1,0:T(8,128)S(1)} collective-permute-done((f32[320,128]{1,0:T(8,128)S(1)}, f32[320,128]{1,0:T(8,128)S(1)}, u32[]{:S(2)}, u32[]{:S(2)}) %collective-permute-start.3) | collective-permute-done | bytes 163872 | tf_op jit(solution)/shard_map/ppermute | solution.py:419
  22.9 0.1 collective-permute-start.4
  23.0 1.6 %collective-permute-done.4 = f32[640,128]{1,0:T(8,128)S(1)} collective-permute-done((f32[640,128]{1,0:T(8,128)S(1)}, f32[640,128]{1,0:T(8,128)S(1)}, u32[]{:S(2)}, u32[]{:S(2)}) %collective-permute-start.4) | collective-permute-done | bytes 327712 | tf_op jit(solution)/shard_map/ppermute | solution.py:419
  24.7 47.0 %shard_map.87 = (f32[1,256]{1,0:T(1,128)}, f32[1,192]{1,0:T(1,128)}) custom-call(s32[1]{0:T(128)} %bitcast.me_ref, f32[1280,128]{1,0:T(8,128)S(1)} %constant_dynamic-update-slice_fusion.5.pieces_ref, f32[1536,1536]{1,0:T(8,128)} %operator_hbm.1, f32[64,256]{1,0:T(8,128)S(1)} %get-tuple-element.10.coupled_ref, f32[256,256]{1,0:T(8,128)S(1)} %get-tuple-element.11.factor_ref, ...), custom_call_target="tpu_custom_call" | custom-call | tf_op jit(solution)/shard_map/pallas_call | solution.py:424
  (9 shorter events, 0.1 us)
Async XLA Ops:
  3.2 5.9 %collective-permute-start = (f32[40,128]{1,0:T(8,128)S(1)}, f32[40,128]{1,0:T(8,128)S(1)}, u32[]{:S(2)}, u32[]{:S(2)}) collective-permute-start(f32[40,128]{1,0:T(8,128)S(1)} %get-tuple-element.9), channel_id=1, source_target_pairs={{0,4},{1,5},{2,6},{3,7},{4,0},{5,1},{6,2},{7,3},{8,12},{9,13},{10,... | collective-permute-start | bytes 61448 | tf_op jit(solution)/shard_map/ppermute | solution.py:419
  9.1 4.0 %collective-permute-start.1 = (f32[80,128]{1,0:T(8,128)S(1)}, f32[80,128]{1,0:T(8,128)S(1)}, u32[]{:S(2)}, u32[]{:S(2)}) collective-permute-start(f32[80,128]{1,0:T(8,128)S(1)} %pad_maximum_fusion.2), channel_id=1, source_target_pairs={{0,2},{1,3},{2,0},{3,1},{4,6},{5,7},{6,4},{7,5},{8,10},{9,11},{10,... | collective-permute-start | bytes 122888 | tf_op jit(solution)/shard_map/ppermute | solution.py:419
  13.1 4.4 %collective-permute-start.2 = (f32[160,128]{1,0:T(8,128)S(1)}, f32[160,128]{1,0:T(8,128)S(1)}, u32[]{:S(2)}, u32[]{:S(2)}) collective-permute-start(f32[160,128]{1,0:T(8,128)S(1)} %pad_maximum_fusion.1), channel_id=1, source_target_pairs={{0,1},{1,0},{2,3},{3,2},{4,5},{5,4},{6,7},{7,6},{8,9},{9,8},{10,11... | collective-permute-start | bytes 245768 | tf_op jit(solution)/shard_map/ppermute | solution.py:419
  17.5 5.4 %collective-permute-start.3 = (f32[320,128]{1,0:T(8,128)S(1)}, f32[320,128]{1,0:T(8,128)S(1)}, u32[]{:S(2)}, u32[]{:S(2)}) collective-permute-start(f32[320,128]{1,0:T(8,128)S(1)} %pad_maximum_fusion), channel_id=1, source_target_pairs={{0,16},{8,24},{16,0},{24,8},{1,17},{9,25},{17,1},{25,9},{2,18},{10... | collective-permute-start | bytes 491528 | tf_op jit(solution)/shard_map/ppermute | solution.py:419
  22.9 1.7 %collective-permute-start.4 = (f32[640,128]{1,0:T(8,128)S(1)}, f32[640,128]{1,0:T(8,128)S(1)}, u32[]{:S(2)}, u32[]{:S(2)}) collective-permute-start(f32[640,128]{1,0:T(8,128)S(1)} %get-tuple-element.16), channel_id=1, source_target_pairs={{0,8},{8,0},{16,24},{24,16},{1,9},{9,1},{17,25},{25,17},{2,10},{10... | collective-permute-start | bytes 983048 | tf_op jit(solution)/shard_map/ppermute | solution.py:419

commit v5 on v4

--- a/solution.py
+++ b/solution.py
@@ -108,10 +108,10 @@
                 ]
                 rows = jnp.concatenate(rows, axis=0)
                 high, low = split(rows)
-                left_high, left_low = split(rows.T[8 * near : 8 * groups])
+                left_high, left_low = high[:, 8 * near : 8 * groups], low[:, 8 * near : 8 * groups]
 
                 def plain(x, y):
-                    return lax.dot_general(x, y, (((1,), (0,)), ((), ())), preferred_element_type=F32)
+                    return lax.dot_general(x, y, (((0,), (0,)), ((), ())), preferred_element_type=F32)
 
                 far = plain(left_high, high) + (plain(left_high, low) + plain(left_low, high))
                 done = (lane >= 8 * start) & (lane < 8 * g + 8)
@@ -323,9 +323,9 @@
         spans = [slice(at, min(at + TB, S)) for at in range(NB * (p + 1), S, TB)]
         work = [begin]
         work += [functools.partial(column, i) for i in range(p + 2, panels)]
-        for at, cols in enumerate(spans):
+        for cols in spans:
             work.append(functools.partial(right, cols))
-            work += [functools.partial(tile, rows, cols) for rows in spans[at:]]
+            work.append(functools.partial(tile, slice(cols.start, S), cols))
         return work
 
     work = []

time: 72.1 us -> 70.8 us (0.982)
  Pallas kernels: 48.9 us -> 47.7 us
    pallas_call x1, Pallas kernels: 47 us -> 45.8 us  [shards(): pl.pallas_call(functools.partial(system_kernel, tuple(steps), n, blk), ou...]
where the time goes in v5:
time: 70.8 us; the launch traced here: 70.6 us
  Pallas kernels  47.7 us (67%)
  waiting for transfers between devices  11.4 us (16%)
  starting transfers between devices  9.98 us (14%)
  between operations  1.5 us (2%)
    pallas_call x1, Pallas kernels, shards(): pl.pallas_call(functools.partial(system_kernel, tuple(steps), n, blk), ou...  45.8 us
    ppermute x5, waiting for transfers between devices, shards(): lax.ppermute(gathered, axis, [(i, i ^ 1 << bit) for i in range(width)])  11.4 us
    ppermute x5, starting transfers between devices, shards(): lax.ppermute(gathered, axis, [(i, i ^ 1 << bit) for i in range(width)])  9.98 us
    pallas_call x1, Pallas kernels, shards(): pl.pallas_call(piece_kernel, out_shape=(pltpu.VMEM((size, 2 * capacity),...  1.89 us
  transfers between devices with their start and end apart: 5, of which 5 were waited for; matrix products, arithmetic and copies ran while one was open for 0% of the time, Pallas kernels for 0%

profile of v5, /device:TPU:0, one launch (start us, length us, event | category | flops | bytes accessed | tf_op | source)
XLA Modules:
  0.0 70.6 jit_solution(11805407482151606557)
XLA Ops:
  1.3 1.9 %shard_map.86 = (f32[40,128]{1,0:T(8,128)S(1)}, f32[64,256]{1,0:T(8,128)S(1)}, f32[256,256]{1,0:T(8,128)S(1)}, f32[1,256]{1,0:T(1,128)S(1)}, f32[12,128]{1,0:T(8,128)S(1)}) custom-call(s32[1]{0:T(128)S(6)} %copy.18.count_ref, f32[64,256]{1,0:T(8,128)} %bitcast.5, f32[256,256]{1,0:T(8,128)} %bitcast.4, f32[1,256]{1,0:T(1,128)} %resid_ref.1, ...), custom_call_target="tpu_custom_call" | custom-call | tf_op jit(solution)/shard_map/pallas_call | solution.py:402
  3.2 4.1 %collective-permute-start = (f32[40,128]{1,0:T(8,128)S(1)}, f32[40,128]{1,0:T(8,128)S(1)}, u32[]{:S(2)}, u32[]{:S(2)}) collective-permute-start(f32[40,128]{1,0:T(8,128)S(1)} %get-tuple-element.9), channel_id=1, source_target_pairs={{0,4},{1,5},{2,6},{3,7},{4,0},{5,1},{6,2},{7,3},{8,12},{9,13},{10,... | collective-permute-start | bytes 61448 | tf_op jit(solution)/shard_map/ppermute | solution.py:419
  7.3 1.8 %collective-permute-done = f32[40,128]{1,0:T(8,128)S(1)} collective-permute-done((f32[40,128]{1,0:T(8,128)S(1)}, f32[40,128]{1,0:T(8,128)S(1)}, u32[]{:S(2)}, u32[]{:S(2)}) %collective-permute-start) | collective-permute-done | bytes 20512 | tf_op jit(solution)/shard_map/ppermute | solution.py:419
  9.1 1.9 %collective-permute-start.1 = (f32[80,128]{1,0:T(8,128)S(1)}, f32[80,128]{1,0:T(8,128)S(1)}, u32[]{:S(2)}, u32[]{:S(2)}) collective-permute-start(f32[80,128]{1,0:T(8,128)S(1)} %pad_maximum_fusion.2), channel_id=1, source_target_pairs={{0,2},{1,3},{2,0},{3,1},{4,6},{5,7},{6,4},{7,5},{8,10},{9,11},{10,... | collective-permute-start | bytes 122888 | tf_op jit(solution)/shard_map/ppermute | solution.py:419
  11.0 2.1 %collective-permute-done.1 = f32[80,128]{1,0:T(8,128)S(1)} collective-permute-done((f32[80,128]{1,0:T(8,128)S(1)}, f32[80,128]{1,0:T(8,128)S(1)}, u32[]{:S(2)}, u32[]{:S(2)}) %collective-permute-start.1) | collective-permute-done | bytes 40992 | tf_op jit(solution)/shard_map/ppermute | solution.py:419
  13.1 1.9 %collective-permute-start.2 = (f32[160,128]{1,0:T(8,128)S(1)}, f32[160,128]{1,0:T(8,128)S(1)}, u32[]{:S(2)}, u32[]{:S(2)}) collective-permute-start(f32[160,128]{1,0:T(8,128)S(1)} %pad_maximum_fusion.1), channel_id=1, source_target_pairs={{0,1},{1,0},{2,3},{3,2},{4,5},{5,4},{6,7},{7,6},{8,9},{9,8},{10,11... | collective-permute-start | bytes 245768 | tf_op jit(solution)/shard_map/ppermute | solution.py:419
  15.0 2.5 %collective-permute-done.2 = f32[160,128]{1,0:T(8,128)S(1)} collective-permute-done((f32[160,128]{1,0:T(8,128)S(1)}, f32[160,128]{1,0:T(8,128)S(1)}, u32[]{:S(2)}, u32[]{:S(2)}) %collective-permute-start.2) | collective-permute-done | bytes 81952 | tf_op jit(solution)/shard_map/ppermute | solution.py:419
  17.5 2.0 %collective-permute-start.3 = (f32[320,128]{1,0:T(8,128)S(1)}, f32[320,128]{1,0:T(8,128)S(1)}, u32[]{:S(2)}, u32[]{:S(2)}) collective-permute-start(f32[320,128]{1,0:T(8,128)S(1)} %pad_maximum_fusion), channel_id=1, source_target_pairs={{0,16},{8,24},{16,0},{24,8},{1,17},{9,25},{17,1},{25,9},{2,18},{10... | collective-permute-start | bytes 491528 | tf_op jit(solution)/shard_map/ppermute | solution.py:419
  19.5 3.4 %collective-permute-done.3 = f32[320,128]{1,0:T(8,128)S(1)} collective-permute-done((f32[320,128]{1,0:T(8,128)S(1)}, f32[320,128]{1,0:T(8,128)S(1)}, u32[]{:S(2)}, u32[]{:S(2)}) %collective-permute-start.3) | collective-permute-done | bytes 163872 | tf_op jit(solution)/shard_map/ppermute | solution.py:419
  22.9 0.1 collective-permute-start.4
  23.0 1.6 %collective-permute-done.4 = f32[640,128]{1,0:T(8,128)S(1)} collective-permute-done((f32[640,128]{1,0:T(8,128)S(1)}, f32[640,128]{1,0:T(8,128)S(1)}, u32[]{:S(2)}, u32[]{:S(2)}) %collective-permute-start.4) | collective-permute-done | bytes 327712 | tf_op jit(solution)/shard_map/ppermute | solution.py:419
  24.7 45.8 %shard_map.87 = (f32[1,256]{1,0:T(1,128)}, f32[1,192]{1,0:T(1,128)}) custom-call(s32[1]{0:T(128)} %bitcast.me_ref, f32[1280,128]{1,0:T(8,128)S(1)} %constant_dynamic-update-slice_fusion.5.pieces_ref, f32[1536,1536]{1,0:T(8,128)} %operator_hbm.1, f32[64,256]{1,0:T(8,128)S(1)} %get-tuple-element.10.coupled_ref, f32[256,256]{1,0:T(8,128)S(1)} %get-tuple-element.11.factor_ref, ...), custom_call_target="tpu_custom_call" | custom-call | tf_op jit(solution)/shard_map/pallas_call | solution.py:424
  (9 shorter events, 0.1 us)
Async XLA Ops:
  3.2 5.9 %collective-permute-start = (f32[40,128]{1,0:T(8,128)S(1)}, f32[40,128]{1,0:T(8,128)S(1)}, u32[]{:S(2)}, u32[]{:S(2)}) collective-permute-start(f32[40,128]{1,0:T(8,128)S(1)} %get-tuple-element.9), channel_id=1, source_target_pairs={{0,4},{1,5},{2,6},{3,7},{4,0},{5,1},{6,2},{7,3},{8,12},{9,13},{10,... | collective-permute-start | bytes 61448 | tf_op jit(solution)/shard_map/ppermute | solution.py:419
  9.1 4.0 %collective-permute-start.1 = (f32[80,128]{1,0:T(8,128)S(1)}, f32[80,128]{1,0:T(8,128)S(1)}, u32[]{:S(2)}, u32[]{:S(2)}) collective-permute-start(f32[80,128]{1,0:T(8,128)S(1)} %pad_maximum_fusion.2), channel_id=1, source_target_pairs={{0,2},{1,3},{2,0},{3,1},{4,6},{5,7},{6,4},{7,5},{8,10},{9,11},{10,... | collective-permute-start | bytes 122888 | tf_op jit(solution)/shard_map/ppermute | solution.py:419
  13.1 4.4 %collective-permute-start.2 = (f32[160,128]{1,0:T(8,128)S(1)}, f32[160,128]{1,0:T(8,128)S(1)}, u32[]{:S(2)}, u32[]{:S(2)}) collective-permute-start(f32[160,128]{1,0:T(8,128)S(1)} %pad_maximum_fusion.1), channel_id=1, source_target_pairs={{0,1},{1,0},{2,3},{3,2},{4,5},{5,4},{6,7},{7,6},{8,9},{9,8},{10,11... | collective-permute-start | bytes 245768 | tf_op jit(solution)/shard_map/ppermute | solution.py:419
  17.5 5.4 %collective-permute-start.3 = (f32[320,128]{1,0:T(8,128)S(1)}, f32[320,128]{1,0:T(8,128)S(1)}, u32[]{:S(2)}, u32[]{:S(2)}) collective-permute-start(f32[320,128]{1,0:T(8,128)S(1)} %pad_maximum_fusion), channel_id=1, source_target_pairs={{0,16},{8,24},{16,0},{24,8},{1,17},{9,25},{17,1},{25,9},{2,18},{10... | collective-permute-start | bytes 491528 | tf_op jit(solution)/shard_map/ppermute | solution.py:419
  22.9 1.7 %collective-permute-start.4 = (f32[640,128]{1,0:T(8,128)S(1)}, f32[640,128]{1,0:T(8,128)S(1)}, u32[]{:S(2)}, u32[]{:S(2)}) collective-permute-start(f32[640,128]{1,0:T(8,128)S(1)} %get-tuple-element.16), channel_id=1, source_target_pairs={{0,8},{8,0},{16,24},{24,16},{1,9},{9,1},{17,25},{25,17},{2,10},{10... | collective-permute-start | bytes 983048 | tf_op jit(solution)/shard_map/ppermute | solution.py:419
